TPU v7x, 256 devices: a whole 4x4x8 slice. The times are simulated.
256 devices in a mesh: req: 8 (over z), shard: 32 (over x, y, core).
Axes of the slice: x: 4, y: 4, z: 8, core: 2. Of those that a mesh axis runs over, the one named last changes fastest.
Arguments:
- paged_key_store: bfloat16 [2816, 16, 1024], P(('req', 'shard')), parts along dimension 0, may hold values from -6 to 6
- paged_value_store: bfloat16 [2816, 16, 1024], P(('req', 'shard')), parts along dimension 0, may hold values from -6 to 6
- paged_scale_store: float32 [2816, 2, 8], P(('req', 'shard')), parts along dimension 0, may hold values from 0.5 to 2
- page_map: int32 [2816], P('req'), parts along dimension 0, may hold values from 0 to 351, each once
- span_order: int32 [64], P('req'), parts along dimension 0, may hold values from 0 to 7, each once
- listed_count: int32 [256], P('req'), parts along dimension 0, may hold values from 4 to 48, as said below
- listed_index: int32 [12288], P('req'), parts along dimension 0, may hold values from 0 to 175, as said below
- listed_queries: bfloat16 [12288, 8192], P(('req', 'shard')), parts along dimension 0, may hold values from -440 to 440
- selected_token_keys: bfloat16 [12288, 1024], P(('req', 'shard')), parts along dimension 0, may hold values from -4.25 to 4.25
- selected_token_values: bfloat16 [12288, 1024], P(('req', 'shard')), parts along dimension 0, may hold values from -6 to 6
Outputs:
- mixed_cache_keys: bfloat16 [2816, 16, 1024], P(('req', 'shard')), parts along dimension 0
- mixed_cache_values: bfloat16 [2816, 16, 1024], P(('req', 'shard')), parts along dimension 0
- attended: bfloat16 [12288, 8192], P(('req', 'shard')), parts along dimension 0
There are 8 independent parts, one for each index of `req`. A program takes and returns all parts, laid end to end along the dimension named above; each array names one. Nothing has to cross between parts.
Inputs may be any that keep to these rules, and one draw needn't show every extreme that they name: `listed_count`: at least 4 on every token shard, exactly 48 on some shard, 26 per shard on average. `listed_index`: the 48 entries of one token shard are distinct; only the first listed_count of them are listed.
All inputs are finite; a program needn't handle non-finite values.
Results may differ from a plain program's by a relative error of at most 0.006.
The roundings to bfloat16 on the way count: a program that leaves them out, or rounds other values in their place, can miss the bound.
Values may be sent and summed in bfloat16 or wider, within the bound.
No kernel may reach another device: no remote copies, remote signals or barrier semaphores. Data moves between devices by JAX's collectives and lax.ppermute only.
A program may use at most 128 MiB of HBM per device.

v0:
```python
import jax
import jax.numpy as jnp
from jax import lax
from jax.sharding import PartitionSpec as P

HEAD_DIMENSION = 128
SPAN_LEN = 704


rope_base = 1000000.0


def apply_rotation(vectors, position):
    half_size = vectors.shape[-1] // 2
    frequency = rope_base ** (-(jnp.arange(half_size, dtype=jnp.float32) * 2.0) / vectors.shape[-1])
    angles = position[..., None].astype(jnp.float32) * frequency
    cosine = jnp.cos(angles)
    sine_part = jnp.sin(angles)
    first_half = vectors[..., :half_size]
    second_half = vectors[..., half_size:]
    return jnp.concatenate(
        [
            first_half * cosine - second_half * sine_part,
            second_half * cosine + first_half * sine_part,
        ],
        axis=-1,
    )


def layout_tables(
    page_map, span_order, listed_count, listed_index, page_token_count, span_size, shard_tokens
):
    stored_page_count = page_map.shape[0]
    span_count = span_order.shape[0]
    per_span = span_size // page_token_count
    shard_count = listed_count.shape[0]
    row_cap = listed_index.shape[0] // shard_count
    logical = (
        jnp.zeros((stored_page_count,), jnp.int32)
        .at[page_map]
        .set(jnp.arange(stored_page_count, dtype=jnp.int32))
    )
    slot_of = (
        jnp.zeros((span_count,), jnp.int32)
        .at[span_order]
        .set(jnp.arange(span_count, dtype=jnp.int32))
    )
    row_shift = slot_of[logical // per_span] * span_size
    row_start = row_shift + logical % per_span * page_token_count
    key_position = (
        row_start[:, None] + jnp.arange(page_token_count, dtype=jnp.int32)[None, :]
    ).reshape(-1)
    selected_token_position = (
        jnp.arange(shard_count, dtype=jnp.int32)[:, None] * shard_tokens
        + listed_index.reshape(shard_count, row_cap)
    ).reshape(-1)
    listed_valid = (jnp.arange(row_cap, dtype=jnp.int32)[None, :] < listed_count[:, None]).reshape(
        -1
    )
    span_slot = selected_token_position // span_size
    within_span = selected_token_position % span_size
    stored_row = page_map[span_order[span_slot] * per_span + within_span // page_token_count]
    cache_index = stored_row * page_token_count + within_span % page_token_count
    return (row_shift, key_position, selected_token_position, listed_valid, cache_index)


def block_rows():
    for candidate in (512, 256, 128, 64, 32, 16, 8, 4, 2):
        return candidate
    return 1


def empty_state(head_count, row_count, head_size):
    return (
        jnp.full((head_count, row_count), -1e30, jnp.float32),
        jnp.zeros((head_count, row_count), jnp.float32),
        jnp.zeros((head_count, row_count, head_size), jnp.float32),
    )


def attend_keys(state, query_rows, query_position, keys, values, key_position):
    length = keys.shape[0]
    block = block_rows()
    steps = length // block
    score_scale = query_rows.shape[-1] ** (-0.5)
    key_blocks = keys.reshape(steps, block, keys.shape[1], keys.shape[2])
    value_blocks = values.reshape(steps, block, values.shape[1], values.shape[2])
    position_blocks = key_position.reshape(steps, block)

    def absorb(carry, operands):
        running_max, running_total, running_sum = carry
        block_keys, block_values, block_position = operands
        scores = (
            jnp.einsum("hrd,phd->hrp", query_rows, block_keys, preferred_element_type=jnp.float32)
            * score_scale
        )
        visible = block_position[None, None, :] <= query_position[None, :, None]
        new_max = jnp.maximum(running_max, jnp.max(jnp.where(visible, scores, -1e30), axis=2))
        factor = jnp.exp(running_max - new_max)
        exps = jnp.where(visible, jnp.exp(scores - new_max[..., None]), 0.0)
        new_total = running_total * factor + jnp.sum(exps, axis=2)
        new_sum = running_sum * factor[..., None] + jnp.einsum(
            "hrp,phd->hrd",
            exps.astype(jnp.bfloat16),
            block_values,
            preferred_element_type=jnp.float32,
        )
        return ((new_max, new_total, new_sum), None)

    return lax.scan(absorb, state, (key_blocks, value_blocks, position_blocks))[0]


def finish(state):
    running_max, running_total, running_sum = state
    return running_sum / jnp.where(running_total > 0, running_total, 1.0)[..., None]


def shards(
    paged_key_store,
    paged_value_store,
    paged_scale_store,
    page_map,
    span_order,
    listed_count,
    listed_index,
    listed_queries,
    selected_token_keys,
    selected_token_values,
):
    my_index = lax.axis_index("shard")
    own_pages, page_token_count, key_value_width = paged_key_store.shape
    kv_heads = key_value_width // HEAD_DIMENSION
    query_heads = listed_queries.shape[1] // HEAD_DIMENSION
    query_group_width = query_heads // kv_heads
    row_cap = listed_queries.shape[0]
    shard_tokens = own_pages * page_token_count
    row_shift, key_position, selected_token_position, listed_valid, cache_index = layout_tables(
        page_map, span_order, listed_count, listed_index, page_token_count, SPAN_LEN, shard_tokens
    )
    own_shift = lax.dynamic_slice_in_dim(row_shift, my_index * own_pages, own_pages)
    dequantized_rows = (
        paged_key_store.astype(jnp.float32).reshape(
            own_pages, page_token_count, kv_heads, HEAD_DIMENSION
        )
        * paged_scale_store[:, 0, None, :, None]
    )
    cached_keys = (
        apply_rotation(dequantized_rows, own_shift[:, None, None])
        .astype(jnp.bfloat16)
        .reshape(shard_tokens, key_value_width)
    )
    stored_value_rows = (
        (
            paged_value_store.astype(jnp.float32).reshape(
                own_pages, page_token_count, kv_heads, HEAD_DIMENSION
            )
            * paged_scale_store[:, 1, None, :, None]
        )
        .astype(jnp.bfloat16)
        .reshape(shard_tokens, key_value_width)
    )
    my_position = lax.dynamic_slice_in_dim(selected_token_position, my_index * row_cap, row_cap)
    my_valid = lax.dynamic_slice_in_dim(listed_valid, my_index * row_cap, row_cap)
    recomputed_key_rows = (
        apply_rotation(
            selected_token_keys.astype(jnp.float32).reshape(row_cap, kv_heads, HEAD_DIMENSION),
            my_position[:, None],
        )
        .astype(jnp.bfloat16)
        .reshape(row_cap, key_value_width)
    )
    query_rows = apply_rotation(
        listed_queries.astype(jnp.float32).reshape(row_cap, query_heads, HEAD_DIMENSION),
        my_position[:, None],
    ).astype(jnp.bfloat16)
    all_keys, all_values = (
        lax.all_gather(recomputed_key_rows, "shard", axis=0, tiled=True),
        lax.all_gather(selected_token_values, "shard", axis=0, tiled=True),
    )
    local_slot = cache_index - my_index * shard_tokens
    picked = (
        local_slot[None, :] == jnp.arange(shard_tokens, dtype=jnp.int32)[:, None]
    ) & listed_valid[None, :]
    chosen_rows = picked.astype(jnp.bfloat16)
    held = jnp.any(picked, axis=1)[:, None]
    swapped_keys = jnp.dot(chosen_rows, all_keys, preferred_element_type=jnp.float32).astype(
        jnp.bfloat16
    )
    swapped_values = jnp.dot(chosen_rows, all_values, preferred_element_type=jnp.float32).astype(
        jnp.bfloat16
    )
    mixed_cache_keys = jnp.where(held, swapped_keys, cached_keys)
    mixed_cache_values = jnp.where(held, swapped_values, stored_value_rows)
    used_keys, used_values = (mixed_cache_keys, mixed_cache_values)
    grouped = (
        query_rows.reshape(row_cap, kv_heads, query_group_width, HEAD_DIMENSION)
        .transpose(1, 0, 2, 3)
        .reshape(kv_heads, row_cap * query_group_width, HEAD_DIMENSION)
    )
    grouped_position = jnp.repeat(jnp.where(my_valid, my_position, -1), query_group_width)
    piece_keys = lax.all_gather(used_keys, "shard", axis=0, tiled=True)
    piece_values = lax.all_gather(used_values, "shard", axis=0, tiled=True)
    length = piece_keys.shape[0]
    state = attend_keys(
        empty_state(kv_heads, row_cap * query_group_width, HEAD_DIMENSION),
        grouped,
        grouped_position,
        piece_keys.reshape(length, kv_heads, HEAD_DIMENSION),
        piece_values.reshape(length, kv_heads, HEAD_DIMENSION),
        key_position,
    )
    result = (
        finish(state)
        .reshape(kv_heads, row_cap, query_group_width, HEAD_DIMENSION)
        .transpose(1, 0, 2, 3)
        .reshape(row_cap, query_heads * HEAD_DIMENSION)
        .astype(jnp.bfloat16)
    )
    return (
        mixed_cache_keys.reshape(own_pages, page_token_count, key_value_width),
        mixed_cache_values.reshape(own_pages, page_token_count, key_value_width),
        result,
    )


def solution(mesh):
    in_specs = (
        P(("req", "shard"), None, None),
        P(("req", "shard"), None, None),
        P(("req", "shard"), None, None),
        P("req"),
        P("req"),
        P("req"),
        P("req"),
        P(("req", "shard"), None),
        P(("req", "shard"), None),
        P(("req", "shard"), None),
    )
    out_specs = (
        P(("req", "shard"), None, None),
        P(("req", "shard"), None, None),
        P(("req", "shard"), None),
    )
    return jax.shard_map(shards, mesh=mesh, in_specs=in_specs, out_specs=out_specs, check_vma=False)
```

profile of v0, /device:TPU:1, one launch (start us, length us, event | category | flops | bytes accessed | tf_op | source)
XLA Modules:
  0.0 424.3 jit_solution(4084382739936914638)
XLA Ops:
  7.3 1.6 fusion.47
  9.0 0.7 iota_compare_fusion.1
  9.9 0.9 convert_bitcast_fusion.1
  10.9 5.8 %compare_select_fusion.1 = (s32[1536]{0:T(1024)S(1)}, s32[1536]{0:T(1024)S(1)}) fusion(s32[]{:T(128)} %bitcast, s32[]{:T(128)} %bitcast.1, s32[]{:T(128)} %bitcast.2, s32[]{:T(128)} %bitcast.3, s32[]{:T(128)} %bitcast.4, s32[]{:T(128)} %bitcast.5, s32[]{:T(128)} %bitcast.6, s32[]{:T(128)} %bitcast.7, s32[1536]{0:T(1024)S(1)} %add.114, s32[1536]{0:T(1024)} %param.18), kind=kLoop, calls=%fused_computation.66 | loop fusion | flops 76800 | bytes 24608 | tf_op jit(solution)/shard_map/select_n | solution.py:62
  17.9 0.7 all-gather.7.cloned.1.call-update
  19.5 9.5 %gather_fusion = s32[1536]{0:T(1024)S(1)} fusion(s32[352]{0:T(512)S(1)} %copy-done, s32[2048]{0:T(1024)S(1)} %pad_clamp_fusion), kind=kCustom, calls=%fused_computation | custom fusion | bytes 18432 | tf_op jit(solution)/shard_map/gather | solution.py:62
  29.0 2.9 scatter_custom_fusion.1
  32.6 5.2 %fusion.40 = (s32[352]{0:T(512)S(1)}, s32[352]{0:T(512)S(1)}) fusion(s32[352]{0:T(512)S(1)} %scatter_custom_fusion.1, s32[]{:T(128)} %bitcast.16, s32[]{:T(128)} %bitcast.15, s32[]{:T(128)} %bitcast.14, s32[]{:T(128)} %bitcast.13, s32[]{:T(128)} %bitcast.12, s32[]{:T(128)} %bitcast.11, s32[]{:T(128)} %bitcast.10, s32[]{:T(128)} %bitcast.9), kind=kLoop, calls=%fused_computation.98 | loop fusion | flops 11264 | bytes 4256 | tf_op jit(solution)/shard_map/add | solution.py:49
  38.9 33.4 %all-gather.5.cloned.1.call-done = bf16[1536,1024]{1,0:T(8,128)(2,1)} async-done(((bf16[48,1024]{1,0:T(8,128)(2,1)}), bf16[1536,1024]{1,0:T(8,128)(2,1)}) %all-gather.5.cloned.1.call-update) | async-done | bytes 3145744 | tf_op jit(solution)/shard_map/all_gather | solution.py:177
  72.3 3.4 fusion.20
  76.1 48.3 %all-gather.7.cloned.1.call-done = bf16[1536,1024]{1,0:T(8,128)(2,1)} async-done(((bf16[48,1024]{1,0:T(8,128)(2,1)}), bf16[1536,1024]{1,0:T(8,128)(2,1)}) %all-gather.7.cloned.1.call-update) | async-done | bytes 3145744 | tf_op jit(solution)/shard_map/all_gather | solution.py:178
  124.6 3.5 fusion.21
  128.9 0.7 fusion.26
  129.7 1.3 copy_bitcast_fusion.5
  131.0 61.4 %all-gather.9.cloned.1.call-done = bf16[5632,1024]{1,0:T(8,128)(2,1)} async-done(((bf16[176,1024]{1,0:T(8,128)(2,1)}), bf16[5632,1024]{1,0:T(8,128)(2,1)}) %all-gather.9.cloned.1.call-update) | async-done | bytes 11534352 | tf_op jit(solution)/shard_map/all_gather | solution.py:201
  192.4 11.1 %copy.47 = bf16[704,8,8,128]{3,2,1,0:T(8,128)(2,1)} copy(bf16[704,8,8,128]{3,1,2,0:T(8,128)(2,1)} %bitcast.121) | data formatting | bytes 23068672
  203.5 56.9 %all-gather.11.cloned.1.call-done = bf16[5632,1024]{1,0:T(8,128)(2,1)} async-done(((bf16[176,1024]{1,0:T(8,128)(2,1)}), bf16[5632,1024]{1,0:T(8,128)(2,1)}) %all-gather.11.cloned.1.call-update) | async-done | bytes 11534352 | tf_op jit(solution)/shard_map/all_gather | solution.py:202
  260.4 11.1 %copy.49 = bf16[704,8,8,128]{3,2,1,0:T(8,128)(2,1)} copy(bf16[704,8,8,128]{3,1,2,0:T(8,128)(2,1)} %bitcast.122) | data formatting | bytes 23068672
  271.5 144.1 %while.15 = (s32[]{:T(128)}, f32[8,384]{1,0:T(8,128)S(1)}, f32[8,384]{1,0:T(8,128)S(1)}, f32[8,384,128]{2,1,0:T(8,128)S(1)}, s32[11,512]{1,0:T(8,128)S(1)}, /*in...) while((s32[]{:T(128)}, f32[8,384]{1,0:T(8,128)S(1)}, ...), condition=%wide.region_6.7_spmd.clone, body=%wide.region_3.6_spmd.clone.sunk | while | flops 823999488 | bytes 58405240 | solution.py:110
  271.9 1.8 constant_dynamic-slice_fusion.6
  273.7 3.8 fusion.59
  277.5 4.2 fusion.60
  282.1 2.5 fusion.62
  285.0 1.8 constant_dynamic-slice_fusion.6
  286.8 3.9 fusion.59
  290.6 4.2 fusion.60
  295.2 2.5 fusion.62
  298.1 1.8 constant_dynamic-slice_fusion.6
  299.9 3.9 fusion.59
  303.7 4.2 fusion.60
  308.3 2.5 fusion.62
  311.2 1.8 constant_dynamic-slice_fusion.6
  313.0 3.9 fusion.59
  316.8 4.2 fusion.60
  321.4 2.5 fusion.62
  324.3 1.8 constant_dynamic-slice_fusion.6
  326.1 3.9 fusion.59
  329.9 4.2 fusion.60
  334.5 2.5 fusion.62
  337.4 1.8 constant_dynamic-slice_fusion.6
  339.2 3.9 fusion.59
  343.0 4.2 fusion.60
  347.6 2.5 fusion.62
  350.5 1.8 constant_dynamic-slice_fusion.6
  352.3 3.9 fusion.59
  356.1 4.2 fusion.60
  360.7 2.5 fusion.62
  363.6 1.8 constant_dynamic-slice_fusion.6
  365.4 3.9 fusion.59
  369.2 4.2 fusion.60
  373.8 2.5 fusion.62
  376.7 1.8 constant_dynamic-slice_fusion.6
  378.5 3.9 fusion.59
  382.3 4.2 fusion.60
  386.9 2.5 fusion.62
  389.8 1.8 constant_dynamic-slice_fusion.6
  391.6 3.9 fusion.59
  395.4 4.2 fusion.60
  400.0 2.5 fusion.62
  402.9 1.8 constant_dynamic-slice_fusion.6
  404.7 3.9 fusion.59
  408.5 4.2 fusion.60
  413.1 2.5 fusion.62
  416.4 1.4 copy.64
  (184 shorter events, 14.0 us)
Async XLA Ops:
  7.2 11.5 %copy-start.6 = (f32[11,2,8]{0,2,1:T(8,128)S(1)}, f32[11,2,8]{0,2,1:T(8,128)}, u32[]{:S(2)}) copy-start(f32[11,2,8]{0,2,1:T(8,128)} %param.14) | copy-start | bytes 2116
  7.2 11.6 %copy-start.4 = (bf16[11,16,1024]{2,1,0:T(8,128)(2,1)S(1)}, bf16[11,16,1024]{2,1,0:T(8,128)(2,1)}, u32[]{:S(2)}) copy-start(bf16[11,16,1024]{2,1,0:T(8,128)(2,1)} %param.12) | copy-start | bytes 1081348
  7.2 65.1 %all-gather.5.cloned.1.call-start = ((), (), s32[]{:S(2)}) async-start(), calls=%async_computation | async-start | bytes 3244032 | tf_op jit(solution)/shard_map/all_gather | solution.py:177
  9.9 9.0 %copy-start.5 = (s32[8]{0:T(128)S(1)}, s32[8]{0:T(128)}, u32[]{:S(2)}) copy-start(s32[8]{0:T(128)} %param.16) | copy-start | bytes 100
  10.8 8.7 %copy-start = (s32[352]{0:T(512)S(1)}, s32[352]{0:T(512)}, u32[]{:S(2)}) copy-start(s32[352]{0:T(512)} %param.15) | copy-start | bytes 4228
  17.8 106.6 %all-gather.7.cloned.1.call-start = ((), (), s32[]{:S(2)}) async-start(), calls=%async_computation.1 | async-start | bytes 3244032 | tf_op jit(solution)/shard_map/all_gather | solution.py:178
  18.6 173.8 %all-gather.9.cloned.1.call-start = ((), (), s32[]{:S(2)}) async-start(), calls=%async_computation.2 | async-start | bytes 11894784 | tf_op jit(solution)/shard_map/all_gather | solution.py:201
  72.3 52.2 %copy-start.7 = (bf16[11,16,1024]{2,1,0:T(8,128)(2,1)S(1)}, bf16[11,16,1024]{2,1,0:T(8,128)(2,1)}, u32[]{:S(2)}) copy-start(bf16[11,16,1024]{2,1,0:T(8,128)(2,1)} %param.13) | copy-start | bytes 1081348
  75.8 184.6 %all-gather.11.cloned.1.call-start = ((), (), s32[]{:S(2)}) async-start(), calls=%async_computation.3 | async-start | bytes 11894784 | tf_op jit(solution)/shard_map/all_gather | solution.py:202
  124.5 3.6 copy-start.2
  271.9 1.8 copy-start.3
  277.5 4.6 %copy-start.1 = (f32[8,512,384]{2,1,0:T(8,128)S(1)}, f32[8,512,384]{2,1,0:T(8,128)}, u32[]{:S(2)}) copy-start(f32[8,512,384]{2,1,0:T(8,128)} %get-tuple-element.243) | copy-start | bytes 18874372 | tf_op jit(solution)/shard_map/while
  285.0 1.8 copy-start.3
  290.6 4.6 %copy-start.1 = (f32[8,512,384]{2,1,0:T(8,128)S(1)}, f32[8,512,384]{2,1,0:T(8,128)}, u32[]{:S(2)}) copy-start(f32[8,512,384]{2,1,0:T(8,128)} %get-tuple-element.243) | copy-start | bytes 18874372 | tf_op jit(solution)/shard_map/while
  298.1 1.8 copy-start.3
  303.7 4.6 %copy-start.1 = (f32[8,512,384]{2,1,0:T(8,128)S(1)}, f32[8,512,384]{2,1,0:T(8,128)}, u32[]{:S(2)}) copy-start(f32[8,512,384]{2,1,0:T(8,128)} %get-tuple-element.243) | copy-start | bytes 18874372 | tf_op jit(solution)/shard_map/while
  311.2 1.8 copy-start.3
  316.8 4.6 %copy-start.1 = (f32[8,512,384]{2,1,0:T(8,128)S(1)}, f32[8,512,384]{2,1,0:T(8,128)}, u32[]{:S(2)}) copy-start(f32[8,512,384]{2,1,0:T(8,128)} %get-tuple-element.243) | copy-start | bytes 18874372 | tf_op jit(solution)/shard_map/while
  324.3 1.8 copy-start.3
  329.9 4.6 %copy-start.1 = (f32[8,512,384]{2,1,0:T(8,128)S(1)}, f32[8,512,384]{2,1,0:T(8,128)}, u32[]{:S(2)}) copy-start(f32[8,512,384]{2,1,0:T(8,128)} %get-tuple-element.243) | copy-start | bytes 18874372 | tf_op jit(solution)/shard_map/while
  337.4 1.8 copy-start.3
  343.0 4.6 %copy-start.1 = (f32[8,512,384]{2,1,0:T(8,128)S(1)}, f32[8,512,384]{2,1,0:T(8,128)}, u32[]{:S(2)}) copy-start(f32[8,512,384]{2,1,0:T(8,128)} %get-tuple-element.243) | copy-start | bytes 18874372 | tf_op jit(solution)/shard_map/while
  350.5 1.8 copy-start.3
  356.1 4.6 %copy-start.1 = (f32[8,512,384]{2,1,0:T(8,128)S(1)}, f32[8,512,384]{2,1,0:T(8,128)}, u32[]{:S(2)}) copy-start(f32[8,512,384]{2,1,0:T(8,128)} %get-tuple-element.243) | copy-start | bytes 18874372 | tf_op jit(solution)/shard_map/while
  363.6 1.8 copy-start.3
  369.2 4.6 %copy-start.1 = (f32[8,512,384]{2,1,0:T(8,128)S(1)}, f32[8,512,384]{2,1,0:T(8,128)}, u32[]{:S(2)}) copy-start(f32[8,512,384]{2,1,0:T(8,128)} %get-tuple-element.243) | copy-start | bytes 18874372 | tf_op jit(solution)/shard_map/while
  376.7 1.8 copy-start.3
  382.3 4.6 %copy-start.1 = (f32[8,512,384]{2,1,0:T(8,128)S(1)}, f32[8,512,384]{2,1,0:T(8,128)}, u32[]{:S(2)}) copy-start(f32[8,512,384]{2,1,0:T(8,128)} %get-tuple-element.243) | copy-start | bytes 18874372 | tf_op jit(solution)/shard_map/while
  389.8 1.8 copy-start.3
  395.4 4.6 %copy-start.1 = (f32[8,512,384]{2,1,0:T(8,128)S(1)}, f32[8,512,384]{2,1,0:T(8,128)}, u32[]{:S(2)}) copy-start(f32[8,512,384]{2,1,0:T(8,128)} %get-tuple-element.243) | copy-start | bytes 18874372 | tf_op jit(solution)/shard_map/while
  402.9 1.8 copy-start.3
  408.5 4.6 %copy-start.1 = (f32[8,512,384]{2,1,0:T(8,128)S(1)}, f32[8,512,384]{2,1,0:T(8,128)}, u32[]{:S(2)}) copy-start(f32[8,512,384]{2,1,0:T(8,128)} %get-tuple-element.243) | copy-start | bytes 18874372 | tf_op jit(solution)/shard_map/while
Sparse Core Ops, SparseCore 0:
  18.0 54.3 all-gather.4
  74.9 49.5 all-gather.6
  127.5 64.8 all-gather.8
  195.4 64.9 all-gather.10
where the time goes:
time: 425 us; the launch traced here: 424 us
  waiting for transfers between devices  201 us (47%)
  matrix products  76.4 us (18%)
  local copies, waits for them, and re-layouts  66.2 us (16%)
  other arithmetic  65.6 us (15%)
  between operations  14.1 us (3%)
    all_gather x1, waiting for transfers between devices, shards(): piece_keys = lax.all_gather(used_keys, 'shard', axis=0, tiled=True)  61.4 us
    all_gather x1, waiting for transfers between devices, shards(): piece_values = lax.all_gather(used_values, 'shard', axis=0, tiled=True)  56.9 us
    all_gather x1, waiting for transfers between devices, shards(): lax.all_gather(selected_token_values, 'shard', axis=0, tiled=True)  48.3 us
    reduce_sum x11, other arithmetic, absorb(): new_total = running_total * factor + jnp.sum(exps, axis=2)  46.6 us
    dot_general x11, matrix products, absorb(): jnp.einsum('hrd,phd->hrp', query_rows, block_keys, preferred_element_type...  42.3 us
    all_gather x1, waiting for transfers between devices, shards(): lax.all_gather(recomputed_key_rows, 'shard', axis=0, tiled=True)  33.4 us
    dot_general x11, matrix products, absorb(): jnp.einsum('hrp,phd->hrd', exps.astype(jnp.bfloat16), block_values, prefe...  27.2 us
    unnamed x19, local copies, waits for them, and re-layouts  24.7 us
  transfers between devices with their start and end apart: 4, of which 4 were waited for; matrix products, arithmetic and copies ran while one was open for 10% of the time, Pallas kernels for 0%

commit v1 on v0

v1 whole, which is shorter than its diff:
```python
import functools

import jax
import jax.numpy as jnp
import numpy as np
from jax import lax
from jax.experimental import pallas as pl
from jax.experimental.pallas import tpu as pltpu
from jax.sharding import PartitionSpec as P

HEAD = 128
KV_HEADS = 8
SPAN_LEN = 704
ROPE_BASE = 1000000.0
MASKED = -1e30
EXP2_SCALE = float(HEAD**-0.5 / np.log(2.0))

BF16 = jnp.bfloat16
F32 = jnp.float32
I32 = jnp.int32
SMEM = pltpu.SMEM
VMEM = pltpu.VMEM


def rope_frequency():
    half = HEAD // 2
    frequency = ROPE_BASE ** (-(np.arange(half, dtype=np.float64) * 2.0) / HEAD)
    return np.concatenate([frequency, frequency]).astype(np.float32)[None, :]


def rope_tables(position, frequency):
    angles = position * frequency
    lane = lax.broadcasted_iota(I32, angles.shape, 1)
    sine = jnp.sin(angles)
    return jnp.cos(angles), jnp.where(lane < HEAD // 2, -sine, sine)


def rotate(x, cosine, sine):
    return x * cosine + pltpu.roll(x, HEAD // 2, 1) * sine


def params(mib, **more):
    return pltpu.CompilerParams(vmem_limit_bytes=mib * 1024 * 1024, **more)


def prepare_kv_kernel(
    shards,
    me_ref,
    page_map,
    span_order,
    listed_index,
    scale,
    frequency,
    keys,
    values,
    fresh_keys,
    fresh_values,
    out,
    cosine_out,
    sine_out,
    slots,
    positions,
    shift_cos,
    shift_sin,
):
    head = pl.program_id(0)
    me = me_ref[0]
    own_pages, page_tokens, _ = keys.shape
    rows = fresh_keys.shape[0]
    per_span = page_map.shape[0] // span_order.shape[0]
    span_count = span_order.shape[0]
    tokens = own_pages * page_tokens

    @pl.when(head == 0)
    def _():
        first = me * own_pages
        for slot in range(span_count):
            start = span_order[slot] * per_span

            def note(p, carry):
                place = page_map[start + p] - first
                inside = (place >= 0) & (place < own_pages)
                slots[jnp.where(inside, place, own_pages)] = slot
                return carry

            lax.fori_loop(0, per_span, note, 0, unroll=11)
        for c in range(rows):
            position = (me * tokens + listed_index[me * rows + c]).astype(F32)
            positions[c : c + 1, :] = jnp.full((1, HEAD), position, F32)
        cosine_out[...], sine_out[...] = rope_tables(positions[...], frequency[...])
        shift = lax.broadcasted_iota(I32, (span_count, HEAD), 0) * SPAN_LEN
        shift_cos[...], shift_sin[...] = rope_tables(shift.astype(F32), frequency[...])

    for page in range(own_pages):
        slot = slots[page]
        cosine = shift_cos[pl.ds(slot, 1), :]
        sine = shift_sin[pl.ds(slot, 1), :]
        span = slice(page * page_tokens, (page + 1) * page_tokens)
        key = keys[page].astype(F32) * scale[page, 0, head]
        key = rotate(key, cosine, sine).astype(BF16)
        value = (values[page].astype(F32) * scale[page, 1, head]).astype(BF16)
        out[0, span] = key
        out[1, span] = value
        out[2, span] = key
        out[3, span] = value
    key = rotate(fresh_keys[...].astype(F32), cosine_out[...], sine_out[...]).astype(BF16)
    value = fresh_values[...]
    out[0, tokens:] = key
    out[1, tokens:] = value
    out[2, tokens:] = key
    out[3, tokens:] = value


def prepare_kv(
    me, page_map, span_order, listed_index, scale, keys, values, fresh_keys, fresh_values, shards
):
    own_pages, page_tokens, _ = keys.shape
    rows = fresh_keys.shape[0]
    sent = own_pages * page_tokens + rows
    group = shards // KV_HEADS
    smem = pl.BlockSpec(memory_space=SMEM)
    return pl.pallas_call(
        functools.partial(prepare_kv_kernel, shards),
        grid=(KV_HEADS,),
        in_specs=[
            smem,
            smem,
            smem,
            smem,
            smem,
            pl.BlockSpec((1, HEAD), lambda h: (0, 0)),
            pl.BlockSpec((own_pages, page_tokens, HEAD), lambda h: (0, 0, h)),
            pl.BlockSpec((own_pages, page_tokens, HEAD), lambda h: (0, 0, h)),
            pl.BlockSpec((rows, HEAD), lambda h: (0, h)),
            pl.BlockSpec((rows, HEAD), lambda h: (0, h)),
        ],
        out_specs=[
            pl.BlockSpec((group, sent, HEAD), lambda h: (h, 0, 0)),
            pl.BlockSpec((rows, HEAD), lambda h: (0, 0)),
            pl.BlockSpec((rows, HEAD), lambda h: (0, 0)),
        ],
        out_shape=[
            jax.ShapeDtypeStruct((shards, sent, HEAD), BF16),
            jax.ShapeDtypeStruct((rows, HEAD), F32),
            jax.ShapeDtypeStruct((rows, HEAD), F32),
        ],
        scratch_shapes=[
            pltpu.SMEM((own_pages + 1,), I32),
            pltpu.VMEM((rows, HEAD), F32),
            pltpu.VMEM((span_order.shape[0], HEAD), F32),
            pltpu.VMEM((span_order.shape[0], HEAD), F32),
        ],
        compiler_params=params(24),
        cost_estimate=pl.CostEstimate(flops=4000000, bytes_accessed=2800000, transcendentals=0),
        name="prepare_kv",
    )(
        me,
        page_map,
        span_order,
        listed_index,
        scale,
        jnp.asarray(rope_frequency()),
        keys,
        values,
        fresh_keys,
        fresh_values,
    )


def prepare_queries_kernel(queries, cosine, sine, out):
    rows = cosine.shape[0]
    for j in range(out.shape[0]):
        for t in range(2):
            head = 2 * j + t
            x = queries[:, head * HEAD : (head + 1) * HEAD].astype(F32)
            out[j, t * rows : (t + 1) * rows] = rotate(x, cosine[...], sine[...]).astype(BF16)


def prepare_queries(queries, cosine, sine, shards):
    rows, width = queries.shape
    steps = 4
    return pl.pallas_call(
        prepare_queries_kernel,
        grid=(steps,),
        in_specs=[
            pl.BlockSpec((rows, width // steps), lambda h: (0, h)),
            pl.BlockSpec((rows, HEAD), lambda h: (0, 0)),
            pl.BlockSpec((rows, HEAD), lambda h: (0, 0)),
        ],
        out_specs=pl.BlockSpec((shards // steps, 2 * rows, HEAD), lambda h: (h, 0, 0)),
        out_shape=jax.ShapeDtypeStruct((shards, 2 * rows, HEAD), BF16),
        compiler_params=params(24),
        cost_estimate=pl.CostEstimate(flops=4000000, bytes_accessed=1600000, transcendentals=0),
        name="prepare_queries",
    )(queries, cosine, sine)


def plan_kernel(
    page_map,
    span_order,
    listed_count,
    listed_lanes,
    source,
    place,
    tiles,
    tile_count,
    positions,
    select,
):
    shards, wide = listed_lanes.shape
    tokens = select.shape[1]
    rows = wide - tokens
    own_pages = page_map.shape[0] // shards
    page_tokens = tokens // own_pages
    span_count = span_order.shape[0]
    per_span = page_map.shape[0] // span_count

    for slot in range(span_count):
        start = span_order[slot] * per_span

        def note(p, carry):
            stored = page_map[start + p]
            logical = slot * per_span + p
            owner = stored // own_pages
            source[logical] = owner * wide + (stored - owner * own_pages) * page_tokens
            place[stored] = logical * page_tokens
            return carry

        lax.fori_loop(0, per_span, note, 0, unroll=4)

    def list_tiles(shard, filled):
        count = listed_count[shard]
        for k in range(rows // 16):
            tiles[filled] = shard * (rows // 16) + k
            filled = filled + jnp.where(count > 16 * k, 1, 0)
        return filled

    filled = lax.fori_loop(0, shards, list_tiles, 0)
    tile_count[0] = filled
    last = tiles[filled - 1]

    def pad(k, carry):
        tiles[filled + k] = last
        return carry

    lax.fori_loop(0, 8, pad, 0)

    token = lax.broadcasted_iota(I32, (tokens, wide), 0)
    column = lax.broadcasted_iota(I32, (tokens, wide), 1)
    same = token == column
    row_of = lax.broadcasted_iota(I32, (rows, wide), 0) + tokens
    row_pick = row_of == lax.broadcasted_iota(I32, (rows, wide), 1)

    def fill(shard, carry):
        listed = listed_lanes[pl.ds(shard, 1), :]
        fresh = listed == token
        held = jnp.sum(jnp.where(fresh, 1.0, 0.0), axis=1, keepdims=True)
        cached = jnp.where(same, 1.0 - held, 0.0)
        select[shard] = jnp.where(fresh, 1.0, cached).astype(BF16)
        offset = jnp.sum(jnp.where(row_pick, listed.astype(F32), 0.0), axis=1, keepdims=True)
        position = jnp.where(offset < 0.0, -1.0, offset + (shard * tokens).astype(F32))
        start = pl.multiple_of(shard * rows, 16)
        positions[pl.ds(start, rows), :] = jnp.broadcast_to(position.astype(I32), (rows, HEAD))
        return carry

    lax.fori_loop(0, shards, fill, 0)


def plan(page_map, span_order, listed_count, listed_lanes, tokens):
    shards, wide = listed_lanes.shape
    rows = wide - tokens
    smem = pl.BlockSpec(memory_space=SMEM)
    vmem = pl.BlockSpec(memory_space=VMEM)
    pages = page_map.shape[0]
    tile_limit = shards * (rows // 16) + 8
    return pl.pallas_call(
        plan_kernel,
        in_specs=[smem, smem, smem, vmem],
        out_specs=[smem, smem, smem, smem, vmem, vmem],
        out_shape=[
            jax.ShapeDtypeStruct((pages,), I32),
            jax.ShapeDtypeStruct((pages,), I32),
            jax.ShapeDtypeStruct((tile_limit,), I32),
            jax.ShapeDtypeStruct((1,), I32),
            jax.ShapeDtypeStruct((shards * rows, HEAD), I32),
            jax.ShapeDtypeStruct((shards, tokens, wide), BF16),
        ],
        compiler_params=params(24),
        cost_estimate=pl.CostEstimate(flops=20000000, bytes_accessed=4000000, transcendentals=0),
        name="plan",
    )(page_map, span_order, listed_count, listed_lanes)


def blend_kernel(me_ref, source, place, select, received, ordered, returned):
    shards, wide, _ = received.shape
    tokens = select.shape[1]
    own_pages = source.shape[0] // shards
    page_tokens = tokens // own_pages
    flat = received.reshape(shards * wide, HEAD)

    def shard_step(shard, carry):
        pages = []
        for page in range(own_pages):
            start = pl.multiple_of(source[shard * own_pages + page], page_tokens)
            pages.append(flat[pl.ds(start, page_tokens), :])
        pages.append(received[shard, tokens:, :])
        start = pl.multiple_of(shard * tokens, 16)
        mixed = jnp.dot(
            select[shard], jnp.concatenate(pages, axis=0), preferred_element_type=F32
        )
        ordered[pl.ds(start, tokens), :] = mixed.astype(BF16)
        return carry

    lax.fori_loop(0, shards, shard_step, 0)

    returned_pages = returned.shape[1] // page_tokens
    first = ((me_ref[0] // 2) % 2) * (own_pages - returned_pages)

    def return_step(shard, carry):
        for page in range(returned_pages):
            start = pl.multiple_of(place[shard * own_pages + first + page], page_tokens)
            span = slice(page * page_tokens, (page + 1) * page_tokens)
            returned[shard, span] = ordered[pl.ds(start, page_tokens), :]
        return carry

    lax.fori_loop(0, shards, return_step, 0)


def blend(me, source, place, select, received):
    shards, wide, _ = received.shape
    tokens = select.shape[1]
    own_pages = source.shape[0] // shards
    page_tokens = tokens // own_pages
    returned_pages = (own_pages + 1) // 2
    smem = pl.BlockSpec(memory_space=SMEM)
    vmem = pl.BlockSpec(memory_space=VMEM)
    return pl.pallas_call(
        blend_kernel,
        in_specs=[smem, smem, smem, vmem, vmem],
        out_specs=[vmem, vmem],
        out_shape=[
            jax.ShapeDtypeStruct((shards * tokens, HEAD), BF16),
            jax.ShapeDtypeStruct((shards, returned_pages * page_tokens, HEAD), BF16),
        ],
        compiler_params=params(32),
        cost_estimate=pl.CostEstimate(flops=400000000, bytes_accessed=7000000, transcendentals=0),
        name="blend",
    )(me, source, place, select, received)


TILES = 8
CHUNK = 512


def attend_kernel(
    me_ref,
    tiles,
    tile_count,
    positions,
    queries,
    mine,
    other,
    out,
    keys,
    values,
    scores,
    block,
    block_position,
    sems,
):
    length = keys.shape[0]
    rows = queries.shape[1] // 2
    shards = queries.shape[0]
    per_shard = rows // 16
    tokens = length // shards
    half = TILES * 16
    core = me_ref[0] % 2

    @pl.when(core == 0)
    def _():
        pltpu.make_async_copy(mine, keys, sems.at[0]).start()
        pltpu.make_async_copy(other, values, sems.at[1]).start()

    @pl.when(core != 0)
    def _():
        pltpu.make_async_copy(other, keys, sems.at[0]).start()
        pltpu.make_async_copy(mine, values, sems.at[1]).start()

    out[...] = jnp.zeros_like(out)
    pltpu.make_async_copy(mine, keys, sems.at[0]).wait()
    pltpu.make_async_copy(mine, values, sems.at[1]).wait()

    def block_step(b, carry):
        first_tile = b * TILES
        for t in range(TILES):
            tile = tiles[first_tile + t]
            shard = tile // per_shard
            row = pl.multiple_of((tile - shard * per_shard) * 16, 16)
            low = slice(t * 16, (t + 1) * 16)
            high = slice(half + t * 16, half + (t + 1) * 16)
            block[low] = queries[shard, pl.ds(row, 16), :]
            block[high] = queries[shard, pl.ds(rows + row, 16), :]
            position = positions[pl.ds(pl.multiple_of(tile * 16, 16), 16), :]
            block_position[low] = position
            block_position[high] = position
        open_keys = (tiles[first_tile] // per_shard) * tokens
        seen_keys = (tiles[first_tile + TILES - 1] // per_shard + 1) * tokens
        open_chunks = open_keys // CHUNK
        seen_chunks = (seen_keys + CHUNK - 1) // CHUNK
        query = block[...]

        def score(chunk):
            start = pl.multiple_of(chunk * CHUNK, CHUNK)
            products = lax.dot_general(
                query,
                keys[pl.ds(start, CHUNK), :],
                (((1,), (1,)), ((), ())),
                preferred_element_type=F32,
            )
            return products * EXP2_SCALE

        def keep(chunk, found, best):
            scores[chunk] = found
            for lane in range(CHUNK // HEAD):
                best = jnp.maximum(best, found[:, lane * HEAD : (lane + 1) * HEAD])
            return best

        def open_step(chunk, best):
            return keep(chunk, score(chunk), best)

        def edge_step(chunk, best):
            found = score(chunk)
            key_position = chunk * CHUNK + lax.broadcasted_iota(I32, (2 * half, CHUNK), 1)
            row_position = jnp.concatenate([block_position[...]] * (CHUNK // HEAD), axis=1)
            return keep(chunk, jnp.where(key_position <= row_position, found, MASKED), best)

        best = jnp.full((2 * half, HEAD), MASKED, F32)
        best = lax.fori_loop(0, open_chunks, open_step, best)
        best = lax.fori_loop(open_chunks, seen_chunks, edge_step, best)
        row_best = jnp.max(best, axis=1, keepdims=True)

        def weigh(chunk, state):
            total, mixed = state
            start = pl.multiple_of(chunk * CHUNK, CHUNK)
            exps = jnp.exp2(scores[chunk] - row_best)
            for lane in range(CHUNK // HEAD):
                total = total + exps[:, lane * HEAD : (lane + 1) * HEAD]
            mixed = mixed + jnp.dot(
                exps.astype(BF16), values[pl.ds(start, CHUNK), :], preferred_element_type=F32
            )
            return total, mixed

        zero = jnp.zeros((2 * half, HEAD), F32)
        total, mixed = lax.fori_loop(0, seen_chunks, weigh, (zero, zero))
        total = jnp.sum(total, axis=1, keepdims=True)
        result = mixed / jnp.where(total > 0, total, 1.0)
        result = jnp.where(block_position[...] >= 0, result, 0.0).astype(BF16)
        for t in range(TILES):
            tile = tiles[first_tile + t]
            shard = tile // per_shard
            row = pl.multiple_of((tile - shard * per_shard) * 16, 16)
            out[shard, pl.ds(row, 16), :] = result[t * 16 : (t + 1) * 16]
            out[shard, pl.ds(rows + row, 16), :] = result[half + t * 16 : half + (t + 1) * 16]
        return carry

    lax.fori_loop(0, (tile_count[0] + TILES - 1) // TILES, block_step, 0)


def attend(me, tiles, tile_count, positions, queries, mine, other):
    length = mine.shape[0]
    smem = pl.BlockSpec(memory_space=SMEM)
    vmem = pl.BlockSpec(memory_space=VMEM)
    anywhere = pl.BlockSpec(memory_space=pl.ANY)
    block = 2 * TILES * 16
    return pl.pallas_call(
        attend_kernel,
        in_specs=[smem, smem, smem, vmem, vmem, anywhere, anywhere],
        out_specs=vmem,
        out_shape=jax.ShapeDtypeStruct(queries.shape, BF16),
        scratch_shapes=[
            pltpu.VMEM((length, HEAD), BF16),
            pltpu.VMEM((length, HEAD), BF16),
            pltpu.VMEM((length // CHUNK, block, CHUNK), F32),
            pltpu.VMEM((block, HEAD), BF16),
            pltpu.VMEM((block, HEAD), I32),
            pltpu.SemaphoreType.DMA((2,)),
        ],
        compiler_params=params(40),
        cost_estimate=pl.CostEstimate(
            flops=3000000000, bytes_accessed=5000000, transcendentals=6000000
        ),
        name="attend",
    )(me, tiles, tile_count, positions, queries, mine, other)


def place_cache_kernel(received, keys, values):
    own_pages, page_tokens, _ = keys.shape
    shared = received.shape[1] // page_tokens
    for part, target in ((0, keys), (1, values)):
        for page in range(own_pages):
            source, at = (part, page) if page < shared else (2 + part, page - own_pages + shared)
            target[page] = received[source, at * page_tokens : (at + 1) * page_tokens]


def place_cache(received, own_pages, page_tokens):
    shards, sent, _ = received.shape
    group = shards // KV_HEADS
    cache = jax.ShapeDtypeStruct((own_pages, page_tokens, KV_HEADS * HEAD), BF16)
    spec = pl.BlockSpec((own_pages, page_tokens, HEAD), lambda h: (0, 0, h))
    return pl.pallas_call(
        place_cache_kernel,
        grid=(KV_HEADS,),
        in_specs=[pl.BlockSpec((group, sent, HEAD), lambda h: (h, 0, 0))],
        out_specs=[spec, spec],
        out_shape=[cache, cache],
        compiler_params=params(24),
        cost_estimate=pl.CostEstimate(flops=0, bytes_accessed=1500000, transcendentals=0),
        name="place_cache",
    )(received)


def place_attended_kernel(received, out):
    rows = out.shape[0]
    for j in range(received.shape[0]):
        for t in range(2):
            head = 2 * j + t
            out[:, head * HEAD : (head + 1) * HEAD] = received[j, t * rows : (t + 1) * rows]


def place_attended(received):
    shards, sent, _ = received.shape
    steps = 4
    rows, width = sent // 2, shards * 2 * HEAD
    return pl.pallas_call(
        place_attended_kernel,
        grid=(steps,),
        in_specs=[pl.BlockSpec((shards // steps, sent, HEAD), lambda h: (h, 0, 0))],
        out_specs=pl.BlockSpec((rows, width // steps), lambda h: (0, h)),
        out_shape=jax.ShapeDtypeStruct((rows, width), BF16),
        compiler_params=params(24),
        cost_estimate=pl.CostEstimate(flops=0, bytes_accessed=1600000, transcendentals=0),
        name="place_attended",
    )(received)


def exchange(blocks):
    return lax.all_to_all(blocks, "shard", 0, 0)


def shard_program(
    shards,
    paged_key_store,
    paged_value_store,
    paged_scale_store,
    page_map,
    span_order,
    listed_count,
    listed_index,
    listed_queries,
    selected_token_keys,
    selected_token_values,
):
    own_pages, page_tokens, _ = paged_key_store.shape
    rows = listed_queries.shape[0]
    tokens = own_pages * page_tokens
    me = lax.axis_index("shard").astype(I32).reshape(1)

    sent_kv, cosine, sine = prepare_kv(
        me,
        page_map,
        span_order,
        listed_index,
        paged_scale_store,
        paged_key_store,
        paged_value_store,
        selected_token_keys,
        selected_token_values,
        shards,
    )
    received_kv = exchange(sent_kv)
    received_queries = exchange(prepare_queries(listed_queries, cosine, sine, shards))

    listed = jnp.arange(rows, dtype=I32)[None, :] < listed_count[:, None]
    listed_lanes = jnp.where(listed, listed_index.reshape(shards, rows), -1)
    listed_lanes = jnp.pad(listed_lanes, ((0, 0), (tokens, 0)), constant_values=-1)
    source, place, tiles, tile_count, positions, select = plan(
        page_map, span_order, listed_count, listed_lanes, tokens
    )

    mine, returned = blend(me, source, place, select, received_kv)
    other = lax.ppermute(mine, "shard", [(i, i ^ 1) for i in range(shards)])
    received_cache = exchange(returned)
    attended = attend(me, tiles, tile_count, positions, received_queries, mine, other)
    mixed_keys, mixed_values = place_cache(received_cache, own_pages, page_tokens)
    return mixed_keys, mixed_values, place_attended(exchange(attended))


def solution(mesh):
    split = ("req", "shard")
    in_specs = (
        P(split, None, None),
        P(split, None, None),
        P(split, None, None),
        P("req"),
        P("req"),
        P("req"),
        P("req"),
        P(split, None),
        P(split, None),
        P(split, None),
    )
    out_specs = (P(split, None, None), P(split, None, None), P(split, None))
    return jax.shard_map(
        functools.partial(shard_program, mesh.shape["shard"]),
        mesh=mesh,
        in_specs=in_specs,
        out_specs=out_specs,
        check_vma=False,
    )
```

time: 425 us -> 142 us (0.33)
  waiting for transfers between devices: 201 us -> 25.9 us
  matrix products: 76.4 us -> 0 us
  other arithmetic: 65.6 us -> 0.07 us
  Pallas kernels: 0 us -> 60.8 us
  local copies, waits for them, and re-layouts: 66.2 us -> 14.1 us
  starting transfers between devices: 0.34 us -> 21 us
  blocking collectives: 0 us -> 17.2 us
  between operations: 14.1 us -> 0.76 us
    all_gather x4 -> x0, waiting for transfers between devices: 200 us -> none  [the longest x1 61.4 us: shards(): piece_keys = lax.all_gather(used_keys, 'shard', axis=0, tiled=True)]
    dot_general x24 -> x0, matrix products: 76.4 us -> none  [the longest x11 42.3 us: absorb(): jnp.einsum('hrd,phd->hrp', query_rows, block_keys, preferred_element_type...]
    pallas_call x0 -> x7, Pallas kernels: none -> 60.8 us  [the longest x1 36.4 us: attend(): pl.pallas_call(attend_kernel, in_specs=[smem, smem, smem, vmem, vmem, any...]
    reduce_sum x11 -> x0, other arithmetic: 46.6 us -> none  [absorb(): new_total = running_total * factor + jnp.sum(exps, axis=2)]
    all_to_all x0 -> x3, waiting for transfers between devices: none -> 25.9 us  [exchange(): return lax.all_to_all(blocks, 'shard', 0, 0)]
    all_to_all x0 -> x3, starting transfers between devices: none -> 20.2 us  [exchange(): return lax.all_to_all(blocks, 'shard', 0, 0)]
    dynamic_slice x22 -> x0, local copies, waits for them, and re-layouts: 19.4 us -> none  [attend_keys(): lax.scan(absorb, state, (key_blocks, value_blocks, position_blocks))[0]]
    all_to_all x0 -> x1, blocking collectives: none -> 17.2 us  [exchange(): return lax.all_to_all(blocks, 'shard', 0, 0)]
  transfers between devices with their start and end apart: 4 -> 4, of which waited for: 4 -> 2; matrix products, arithmetic and copies ran while one was open for 10% -> 0% of each run, Pallas kernels for 0% -> 34%
where the time goes in v1:
time: 142 us; the launch traced here: 140 us
  Pallas kernels  60.8 us (43%)
  waiting for transfers between devices  25.9 us (18%)
  starting transfers between devices  21 us (15%)
  blocking collectives  17.2 us (12%)
  local copies, waits for them, and re-layouts  14.1 us (10%)
    pallas_call x1, Pallas kernels, attend(): pl.pallas_call(attend_kernel, in_specs=[smem, smem, smem, vmem, vmem, any...  36.4 us
    all_to_all x3, waiting for transfers between devices, exchange(): return lax.all_to_all(blocks, 'shard', 0, 0)  25.9 us
    all_to_all x3, starting transfers between devices, exchange(): return lax.all_to_all(blocks, 'shard', 0, 0)  20.2 us
    all_to_all x1, blocking collectives, exchange(): return lax.all_to_all(blocks, 'shard', 0, 0)  17.2 us
    unnamed x37, local copies, waits for them, and re-layouts  13.9 us
    pallas_call x1, Pallas kernels, plan(): pl.pallas_call(plan_kernel, in_specs=[smem, smem, smem, vmem], out_specs=...  8.45 us
    pallas_call x1, Pallas kernels, blend(): pl.pallas_call(blend_kernel, in_specs=[smem, smem, smem, vmem, vmem], out...  7.67 us
    pallas_call x1, Pallas kernels, prepare_kv(): pl.pallas_call(functools.partial(prepare_kv_kernel, shards), grid=(KV_HEA...  3.52 us
  transfers between devices with their start and end apart: 4, of which 2 were waited for; matrix products, arithmetic and copies ran while one was open for 0% of the time, Pallas kernels for 34%

profile of v1, /device:TPU:1, one launch (start us, length us, event | category | flops | bytes accessed | tf_op | source)
XLA Modules:
  0.0 139.8 jit_solution(2589848629144773548)
XLA Ops:
  0.6 0.8 copy.14.scale
  1.4 0.0 copy-start.4
  1.4 1.0 copy-done.4
  2.4 0.0 copy-start.5
  2.4 1.0 copy-done.5
  3.4 0.0 copy-start.6
  3.4 0.9 copy-done.6
  4.3 0.0 copy-start.7
  4.3 0.9 copy-done.7
  5.2 0.0 copy-start.8
  5.2 0.7 copy-done.8
  5.9 0.0 copy-start.10
  5.9 0.7 copy-done.10
  6.6 0.0 copy-start.12
  6.6 0.7 copy-done.12
  7.2 0.0 copy-start.15
  7.2 0.7 copy-done.15
  7.9 3.5 %prepare_kv.1 = (bf16[32,224,128]{2,1,0:T(8,128)(2,1)S(1)}, f32[48,128]{1,0:T(8,128)S(1)}, f32[48,128]{1,0:T(8,128)S(1)}) custom-call(s32[1]{0:T(128)} %bitcast.me_ref, s32[352]{0:T(512)S(1)} %copy-done.10, s32[8]{0:T(128)S(1)} %copy-done.12, s32[1536]{0:T(1024)S(1)} %copy-done.8, f32[11,2,8]{2,1,0:T(2,128)S(1)} %copy.14.scale, f32[1,128]{1,0:T(1,128)S(1)} %copy-done.15, ...), custom_call_target="tpu_custom_call" | custom-call | flops 4000000 | bytes 2800000 | tf_op jit(solution)/shard_map/prepare_kv/pallas_call | solution.py:122
  11.4 0.0 copy-start.2
  11.4 1.3 copy-done.2
  12.7 0.0 copy-start.9
  12.7 0.0 copy-start.14
  12.7 0.0 copy-start.11
  12.7 0.0 copy-start.13
  12.7 8.7 %all-to-all-start = ((bf16[32,224,128]{2,1,0:T(8,128)(2,1)}), bf16[32,224,128]{2,1,0:T(8,128)(2,1)S(1)}, u32[]{:S(2)}, u32[]{:S(2)}) async-start(bf16[32,224,128]{2,1,0:T(8,128)(2,1)} %copy-done.2), calls=%async_computation | async-start | bytes 3670016 | tf_op jit(solution)/shard_map/all_to_all | solution.py:547
  21.4 0.0 copy-done.9
  21.4 0.1 reshape.14
  21.5 0.0 copy-done.14
  21.5 0.1 fusion
  21.6 0.1 pad.4.listed_lanes
  21.7 0.0 copy-done.11
  21.7 0.0 copy-done.13
  21.7 8.5 %plan.1 = (s32[352]{0:T(512)S(1)}, s32[352]{0:T(512)S(1)}, s32[104]{0:T(128)S(1)}, s32[1]{0:T(128)}, s32[1536,128]{1,0:T(8,128)S(1)}, /*index=5*/bf16[32,176,224]{2,1,0:T(8,128)(2,1)S(1)}) custom-call(s32[352]{0:T(512)S(1)} %copy-done.11, s32[8]{0:T(128)S(1)} %copy-done.13, s32[32]{0:T(128)S(1)} %copy-done.14, s32[32,224]{1,0:T(8,128)S(1)} %pad.4.listed_lanes), custom_call_target="tpu_custom_call" | custom-call | flops 20000000 | bytes 4000000 | tf_op jit(solution)/shard_map/plan/pallas_call | solution.py:276
  30.1 0.0 copy-start
  30.1 1.5 %copy-done = bf16[32,176,224]{2,1,0:T(8,128)(2,1)} copy-done((bf16[32,176,224]{2,1,0:T(8,128)(2,1)}, bf16[32,176,224]{2,1,0:T(8,128)(2,1)S(1)}, u32[]{:S(2)}) %copy-start) | copy-done | bytes 2523160
  31.7 0.0 copy-start.16
  31.7 0.9 copy-done.16
  32.6 14.3 %all-to-all-done.received = bf16[32,224,128]{2,1,0:T(8,128)(2,1)S(1)} async-done(((bf16[32,224,128]{2,1,0:T(8,128)(2,1)}), bf16[32,224,128]{2,1,0:T(8,128)(2,1)S(1)}, u32[]{:S(2)}, u32[]{:S(2)}) %all-to-all-start) | async-done | bytes 1835040 | tf_op jit(solution)/shard_map/all_to_all | solution.py:547
  46.9 0.0 copy-start.1
  46.9 1.8 %copy-done.1 = bf16[32,176,224]{2,1,0:T(8,128)(2,1)S(1)} copy-done((bf16[32,176,224]{2,1,0:T(8,128)(2,1)S(1)}, bf16[32,176,224]{2,1,0:T(8,128)(2,1)}, u32[]{:S(2)}) %copy-start.1) | copy-done | bytes 2523160
  48.7 0.0 copy-start.3
  48.7 7.7 %blend.1 = (bf16[5632,128]{1,0:T(8,128)(2,1)S(1)}, bf16[32,96,128]{2,1,0:T(8,128)(2,1)}) custom-call(s32[1]{0:T(128)} %bitcast.me_ref, s32[352]{0:T(512)S(1)} %get-tuple-element.16.source, s32[352]{0:T(512)S(1)} %get-tuple-element.17.place, bf16[32,176,224]{2,1,0:T(8,128)(2,1)S(1)} %copy-done.1, bf16[32,224,128]{2,1,0:T(8,128)(2,1)S(1)} %all-to-all-done.received), custom_call_target="tpu_custom_call" | custom-call | flops 400000000 | bytes 7000000 | tf_op jit(solution)/shard_map/blend/pallas_call | solution.py:337
  56.4 0.8 collective-permute-start
  57.2 0.0 copy-done.3
  57.2 0.6 prepare_queries.1
  57.8 17.2 %all_to_all.20.queries = bf16[32,96,128]{2,1,0:T(8,128)(2,1)S(1)} all-to-all(bf16[32,96,128]{2,1,0:T(8,128)(2,1)S(1)} %prepare_queries.1), channel_id=1, replica_groups=mesh['req'=8,'shard'=32] {'shard'}, dimensions={0} | all-to-all | bytes 1572864 | tf_op jit(solution)/shard_map/all_to_all | solution.py:547
  75.0 3.8 %all-to-all-start.1 = ((bf16[32,96,128]{2,1,0:T(8,128)(2,1)}), bf16[32,96,128]{2,1,0:T(8,128)(2,1)S(1)}, u32[]{:S(2)}, u32[]{:S(2)}) async-start(bf16[32,96,128]{2,1,0:T(8,128)(2,1)} %get-tuple-element.20), calls=%async_computation.1 | async-start | bytes 1572864 | tf_op jit(solution)/shard_map/all_to_all | solution.py:547
  78.9 0.0 collective-permute-done.other
  78.9 0.0 copy-start.17
  78.9 1.1 copy-done.17
  80.0 36.4 %attend.1 = bf16[32,96,128]{2,1,0:T(8,128)(2,1)} custom-call(s32[1]{0:T(128)} %bitcast.me_ref, s32[104]{0:T(128)S(1)} %get-tuple-element.23.tiles, s32[1]{0:T(128)} %get-tuple-element.24.tile_count, s32[1536,128]{1,0:T(8,128)S(1)} %copy-done.17, bf16[32,96,128]{2,1,0:T(8,128)(2,1)S(1)} %all_to_all.20.queries, bf16[5632,128]{1,0:T(8,128)(2,1)S(1)} %get-tuple-element.28.mine, ...), custom_call_target="tpu_custom_call" | custom-call | flops 3000000000 | bytes 5000000 | tf_op jit(solution)/shard_map/attend/pallas_call | solution.py:475
  116.4 0.0 all-to-all-done.1.received
  116.4 7.7 %all-to-all-start.3 = ((bf16[32,96,128]{2,1,0:T(8,128)(2,1)}), bf16[32,96,128]{2,1,0:T(8,128)(2,1)S(1)}, u32[]{:S(2)}, u32[]{:S(2)}) async-start(bf16[32,96,128]{2,1,0:T(8,128)(2,1)} %attend.1), calls=%async_computation.3 | async-start | bytes 1572864 | tf_op jit(solution)/shard_map/all_to_all | solution.py:547
  124.1 2.6 %place_cache.1 = (bf16[11,16,1024]{2,1,0:T(8,128)(2,1)}, bf16[11,16,1024]{2,1,0:T(8,128)(2,1)}) custom-call(bf16[32,96,128]{2,1,0:T(8,128)(2,1)S(1)} %all-to-all-done.1.received), custom_call_target="tpu_custom_call" | custom-call | bytes 1500000 | tf_op jit(solution)/shard_map/place_cache/pallas_call | solution.py:510
  126.7 11.6 %all-to-all-done.3.received = bf16[32,96,128]{2,1,0:T(8,128)(2,1)S(1)} async-done(((bf16[32,96,128]{2,1,0:T(8,128)(2,1)}), bf16[32,96,128]{2,1,0:T(8,128)(2,1)S(1)}, u32[]{:S(2)}, u32[]{:S(2)}) %all-to-all-start.3) | async-done | bytes 786464 | tf_op jit(solution)/shard_map/all_to_all | solution.py:547
  138.3 1.5 %place_attended.1 = bf16[48,8192]{1,0:T(8,128)(2,1)} custom-call(bf16[32,96,128]{2,1,0:T(8,128)(2,1)S(1)} %all-to-all-done.3.received), custom_call_target="tpu_custom_call" | custom-call | bytes 1600000 | tf_op jit(solution)/shard_map/place_attended/pallas_call | solution.py:534
Async XLA Ops:
  1.4 1.0 copy-start.4
  2.4 1.0 copy-start.5
  3.4 0.9 copy-start.6
  4.3 0.9 copy-start.7
  5.2 0.7 copy-start.8
  5.9 0.7 copy-start.10
  6.6 0.7 copy-start.12
  7.2 0.7 copy-start.15
  11.4 1.3 copy-start.2
  12.7 8.8 %copy-start.9 = (s32[1536]{0:T(1024)S(1)}, s32[1536]{0:T(1024)}, u32[]{:S(2)}) copy-start(s32[1536]{0:T(1024)} %listed_index.1) | copy-start | bytes 18436
  12.7 8.8 %copy-start.14 = (s32[32]{0:T(128)S(1)}, s32[32]{0:T(128)}, u32[]{:S(2)}) copy-start(s32[32]{0:T(128)} %listed_count.1) | copy-start | bytes 388
  12.7 9.0 %copy-start.11 = (s32[352]{0:T(512)S(1)}, s32[352]{0:T(512)}, u32[]{:S(2)}) copy-start(s32[352]{0:T(512)} %page_map.3) | copy-start | bytes 4228
  12.7 9.0 %copy-start.13 = (s32[8]{0:T(128)S(1)}, s32[8]{0:T(128)}, u32[]{:S(2)}) copy-start(s32[8]{0:T(128)} %span_order.3) | copy-start | bytes 100
  12.7 34.2 %all-to-all-start = ((bf16[32,224,128]{2,1,0:T(8,128)(2,1)}), bf16[32,224,128]{2,1,0:T(8,128)(2,1)S(1)}, u32[]{:S(2)}, u32[]{:S(2)}) async-start(bf16[32,224,128]{2,1,0:T(8,128)(2,1)} %copy-done.2), calls=%async_computation | async-start | bytes 3670016 | tf_op jit(solution)/shard_map/all_to_all | solution.py:547
  30.1 1.5 %copy-start = (bf16[32,176,224]{2,1,0:T(8,128)(2,1)}, bf16[32,176,224]{2,1,0:T(8,128)(2,1)S(1)}, u32[]{:S(2)}) copy-start(bf16[32,176,224]{2,1,0:T(8,128)(2,1)S(1)} %get-tuple-element.18.select) | copy-start | bytes 7569412
  31.7 0.9 copy-start.16
  46.9 1.8 %copy-start.1 = (bf16[32,176,224]{2,1,0:T(8,128)(2,1)S(1)}, bf16[32,176,224]{2,1,0:T(8,128)(2,1)}, u32[]{:S(2)}) copy-start(bf16[32,176,224]{2,1,0:T(8,128)(2,1)} %copy-done) | copy-start | bytes 7569412
  48.7 8.4 %copy-start.3 = (bf16[48,8192]{1,0:T(8,128)(2,1)S(1)}, bf16[48,8192]{1,0:T(8,128)(2,1)}, u32[]{:S(2)}) copy-start(bf16[48,8192]{1,0:T(8,128)(2,1)} %queries.1) | copy-start | bytes 2359300
  56.4 22.5 %collective-permute-start = (bf16[5632,128]{1,0:T(8,128)(2,1)S(1)}, bf16[5632,128]{1,0:T(8,128)(2,1)}, u32[]{:S(2)}, u32[]{:S(2)}) collective-permute-start(bf16[5632,128]{1,0:T(8,128)(2,1)S(1)} %get-tuple-element.28.mine), channel_id=1, source_target_pairs={{0,1},{1,0},{2,3},{3,2},{4,5},{5,4},{6,7},{7,6},{8,9},{9,8},{10,11... | collective-permute-start | bytes 4325384 | tf_op jit(solution)/shard_map/ppermute | solution.py:591
  75.0 41.4 %all-to-all-start.1 = ((bf16[32,96,128]{2,1,0:T(8,128)(2,1)}), bf16[32,96,128]{2,1,0:T(8,128)(2,1)S(1)}, u32[]{:S(2)}, u32[]{:S(2)}) async-start(bf16[32,96,128]{2,1,0:T(8,128)(2,1)} %get-tuple-element.20), calls=%async_computation.1 | async-start | bytes 1572864 | tf_op jit(solution)/shard_map/all_to_all | solution.py:547
  78.9 1.1 copy-start.17
  116.4 21.9 %all-to-all-start.3 = ((bf16[32,96,128]{2,1,0:T(8,128)(2,1)}), bf16[32,96,128]{2,1,0:T(8,128)(2,1)S(1)}, u32[]{:S(2)}, u32[]{:S(2)}) async-start(bf16[32,96,128]{2,1,0:T(8,128)(2,1)} %attend.1), calls=%async_computation.3 | async-start | bytes 1572864 | tf_op jit(solution)/shard_map/all_to_all | solution.py:547

commit v2 on v1

v2 whole, which is shorter than its diff:
```python
import functools

import jax
import jax.numpy as jnp
import numpy as np
from jax import lax
from jax.experimental import pallas as pl
from jax.experimental.pallas import tpu as pltpu
from jax.sharding import PartitionSpec as P

HEAD = 128
KV_HEADS = 8
SPAN_LEN = 704
ROPE_BASE = 1000000.0
MASKED = -1e30
VMEM_MIB = 56
TILES = 16
CHUNK = 1408
TURN = 512
PAGE = 16
EXP2_SCALE = float(HEAD**-0.5 / np.log(2.0))

BF16 = jnp.bfloat16
F32 = jnp.float32
I32 = jnp.int32
SMEM = pltpu.SMEM
VMEM = pltpu.VMEM


def rope_frequency():
    half = HEAD // 2
    frequency = ROPE_BASE ** (-(np.arange(half, dtype=np.float64) * 2.0) / HEAD)
    return np.concatenate([frequency, frequency]).astype(np.float32)[None, :]


def rope_tables(position, frequency):
    angles = position * frequency
    lane = lax.broadcasted_iota(I32, angles.shape, 1)
    sine = jnp.sin(angles)
    return jnp.cos(angles), jnp.where(lane < HEAD // 2, -sine, sine)


def rotate(x, cosine, sine):
    return x * cosine + pltpu.roll(x, HEAD // 2, 1) * sine


def params(mib, **more):
    return pltpu.CompilerParams(vmem_limit_bytes=mib * 1024 * 1024, **more)


def prepare_kernel(
    me_ref,
    page_map,
    span_order,
    listed_index,
    scale,
    frequency,
    queries,
    keys,
    values,
    fresh_keys,
    fresh_values,
    out,
    slots,
    positions,
    row_cos,
    row_sin,
    shift_cos,
    shift_sin,
):
    head = pl.program_id(0)
    me = me_ref[0]
    own_pages, page_tokens, _ = keys.shape
    rows = fresh_keys.shape[0]
    group = out.shape[0]
    span_count = span_order.shape[0]
    per_span = page_map.shape[0] // span_count
    tokens = own_pages * page_tokens

    @pl.when(head == 0)
    def _():
        first = me * own_pages
        for slot in range(span_count):
            start = span_order[slot] * per_span

            def note(p, carry):
                place = page_map[start + p] - first
                inside = (place >= 0) & (place < own_pages)
                slots[jnp.where(inside, place, own_pages)] = slot
                return carry

            lax.fori_loop(0, per_span, note, 0, unroll=11)
        for c in range(rows):
            position = (me * tokens + listed_index[me * rows + c]).astype(F32)
            positions[c : c + 1, :] = jnp.full((1, HEAD), position, F32)
        row_cos[...], row_sin[...] = rope_tables(positions[...], frequency[...])
        shift = lax.broadcasted_iota(I32, (span_count, HEAD), 0) * SPAN_LEN
        shift_cos[...], shift_sin[...] = rope_tables(shift.astype(F32), frequency[...])

    cosine, sine = row_cos[...], row_sin[...]
    for j in range(group):
        for t in range(2):
            at = (2 * j + t) * HEAD
            x = queries[:, at : at + HEAD].astype(F32)
            out[j, t * rows : (t + 1) * rows] = rotate(x, cosine, sine).astype(BF16)
    base = 2 * rows
    for page in range(own_pages):
        slot = slots[page]
        page_cos = shift_cos[pl.ds(slot, 1), :]
        page_sin = shift_sin[pl.ds(slot, 1), :]
        span = slice(base + page * page_tokens, base + (page + 1) * page_tokens)
        key = keys[page].astype(F32) * scale[0, head, page]
        key = rotate(key, page_cos, page_sin).astype(BF16)
        value = (values[page].astype(F32) * scale[1, head, page]).astype(BF16)
        for j in range(group):
            out[j, span] = value if j % 2 else key
    key = rotate(fresh_keys[...].astype(F32), cosine, sine).astype(BF16)
    value = fresh_values[...]
    for j in range(group):
        out[j, base + tokens :] = value if j % 2 else key


def prepare(
    me,
    page_map,
    span_order,
    listed_index,
    scale,
    queries,
    keys,
    values,
    fresh_keys,
    fresh_values,
    shards,
):
    own_pages, page_tokens, _ = keys.shape
    rows, width = queries.shape
    sent = 3 * rows + own_pages * page_tokens
    smem = pl.BlockSpec(memory_space=SMEM)
    pages = pl.BlockSpec((own_pages, page_tokens, HEAD), lambda h: (0, 0, h))
    fresh = pl.BlockSpec((rows, HEAD), lambda h: (0, h))
    return pl.pallas_call(
        prepare_kernel,
        grid=(KV_HEADS,),
        in_specs=[
            smem,
            smem,
            smem,
            smem,
            smem,
            pl.BlockSpec((1, HEAD), lambda h: (0, 0)),
            pl.BlockSpec((rows, width // KV_HEADS), lambda h: (0, h)),
            pages,
            pages,
            fresh,
            fresh,
        ],
        out_specs=pl.BlockSpec((shards // KV_HEADS, sent, HEAD), lambda h: (h, 0, 0)),
        out_shape=jax.ShapeDtypeStruct((shards, sent, HEAD), BF16),
        scratch_shapes=[
            pltpu.SMEM((own_pages + 1,), I32),
            pltpu.VMEM((rows, HEAD), F32),
            pltpu.VMEM((rows, HEAD), F32),
            pltpu.VMEM((rows, HEAD), F32),
            pltpu.VMEM((span_order.shape[0], HEAD), F32),
            pltpu.VMEM((span_order.shape[0], HEAD), F32),
        ],
        compiler_params=params(VMEM_MIB),
        cost_estimate=pl.CostEstimate(
            flops=5000000000, bytes_accessed=4300000, transcendentals=0
        ),
        name="prepare",
    )(
        me,
        page_map,
        span_order,
        listed_index,
        scale,
        jnp.asarray(rope_frequency()),
        queries,
        keys,
        values,
        fresh_keys,
        fresh_values,
    )


def plan_kernel(
    page_map,
    span_order,
    listed_count,
    listed_lanes,
    source,
    place,
    tiles,
    block_count,
    positions,
    row_position,
):
    shards, rows = listed_lanes.shape
    pages = page_map.shape[0]
    own_pages = pages // shards
    page_tokens = PAGE
    tokens = own_pages * page_tokens
    sent = tokens + 3 * rows
    span_count = span_order.shape[0]
    per_span = pages // span_count

    for slot in range(span_count):
        start = span_order[slot] * per_span

        def note(p, carry):
            stored = page_map[start + p]
            logical = slot * per_span + p
            owner = stored // own_pages
            within = stored - owner * own_pages
            source[logical] = owner * sent + 2 * rows + within * page_tokens
            place[stored] = logical * page_tokens
            return carry

        lax.fori_loop(0, per_span, note, 0, unroll=4)

    def count_tiles(shard, total):
        return total + (listed_count[shard] + 15) // 16

    total = lax.fori_loop(0, shards, count_tiles, 0)
    blocks = (total + TILES - 1) // TILES
    block_count[0] = blocks
    for k in range(TILES):
        tiles[k] = 0

    def list_tiles(shard, filled):
        count = listed_count[shard]
        for k in range(rows // 16):
            tiles[filled] = shard * (rows // 16) + k
            filled = filled + jnp.where(count > 16 * k, 1, 0)
        return filled

    lax.fori_loop(0, shards, list_tiles, blocks * TILES - total)

    diagonal = lax.broadcasted_iota(I32, (rows, rows), 0) == lax.broadcasted_iota(
        I32, (rows, rows), 1
    )

    def fill(shard, carry):
        listed = listed_lanes[pl.ds(shard, 1), :].astype(F32)
        offset = jnp.sum(jnp.where(diagonal, listed, 0.0), axis=1, keepdims=True)
        position = jnp.where(offset < 0.0, -1.0, offset + (shard * tokens).astype(F32))
        start = pl.multiple_of(shard * rows, 16)
        row_position[pl.ds(start, rows), :] = jnp.broadcast_to(position, (rows, HEAD))
        return carry

    lax.fori_loop(0, shards, fill, 0)

    def place_positions(b, carry):
        lanes = []
        for t in range(0, TILES, 8):
            found = []
            for u in range(t, t + 8):
                start = pl.multiple_of(tiles[b * TILES + u] * 16, 16)
                found.append(row_position[pl.ds(start, 16), :])
            lanes.append(jnp.concatenate(found, axis=0).T[:8])
        positions[b] = jnp.concatenate(lanes + lanes, axis=1).astype(I32)
        return carry

    lax.fori_loop(0, blocks, place_positions, 0)


def plan(page_map, span_order, listed_count, listed_lanes):
    shards, rows = listed_lanes.shape
    smem = pl.BlockSpec(memory_space=SMEM)
    vmem = pl.BlockSpec(memory_space=VMEM)
    pages = page_map.shape[0]
    block_limit = pl.cdiv(shards * (rows // 16), TILES)
    return pl.pallas_call(
        plan_kernel,
        in_specs=[smem, smem, smem, vmem],
        out_specs=[smem, smem, smem, smem, vmem],
        out_shape=[
            jax.ShapeDtypeStruct((pages,), I32),
            jax.ShapeDtypeStruct((pages,), I32),
            jax.ShapeDtypeStruct(((block_limit + 1) * TILES,), I32),
            jax.ShapeDtypeStruct((1,), I32),
            jax.ShapeDtypeStruct((block_limit, 8, 32 * TILES), I32),
        ],
        scratch_shapes=[pltpu.VMEM((shards * rows, HEAD), F32)],
        compiler_params=params(16),
        cost_estimate=pl.CostEstimate(
            flops=9000000000, bytes_accessed=3000000, transcendentals=0
        ),
        name="plan",
    )(page_map, span_order, listed_count, listed_lanes)


def blend_kernel(me_ref, source, place, listed_lanes, received, ordered, returned):
    shards, sent, _ = received.shape
    rows = listed_lanes.shape[1]
    own_pages = source.shape[0] // shards
    page_tokens = PAGE
    tokens = own_pages * page_tokens
    flat = received.reshape(shards * sent, HEAD)
    token = lax.broadcasted_iota(I32, (tokens, rows), 0)
    ones = jnp.ones((rows, HEAD), BF16)

    def shard_step(shard, carry):
        pages = []
        for page in range(own_pages):
            start = pl.multiple_of(source[shard * own_pages + page], page_tokens)
            pages.append(flat[pl.ds(start, page_tokens), :])
        cached = jnp.concatenate(pages, axis=0)
        pick = jnp.where(listed_lanes[pl.ds(shard, 1), :] == token, 1.0, 0.0).astype(BF16)
        fresh = jnp.concatenate([received[shard, 2 * rows + tokens :, :], ones], axis=1)
        found = jnp.dot(pick, fresh, preferred_element_type=F32)
        mixed = jnp.where(found[:, HEAD:] > 0.5, found[:, :HEAD], cached.astype(F32))
        start = pl.multiple_of(shard * tokens, 16)
        ordered[pl.ds(start, tokens), :] = mixed.astype(BF16)
        return carry

    lax.fori_loop(0, shards, shard_step, 0, unroll=4)

    returned_pages = returned.shape[1] // page_tokens
    first = ((me_ref[0] // 2) % 2) * (own_pages - returned_pages)

    def return_step(shard, carry):
        for page in range(returned_pages):
            start = pl.multiple_of(place[shard * own_pages + first + page], page_tokens)
            span = slice(page * page_tokens, (page + 1) * page_tokens)
            returned[shard, span] = ordered[pl.ds(start, page_tokens), :]
        return carry

    lax.fori_loop(0, shards, return_step, 0, unroll=4)


def blend(me, source, place, listed_lanes, received):
    shards, rows = listed_lanes.shape
    own_pages = source.shape[0] // shards
    returned_pages = (own_pages + 1) // 2
    smem = pl.BlockSpec(memory_space=SMEM)
    vmem = pl.BlockSpec(memory_space=VMEM)
    return pl.pallas_call(
        blend_kernel,
        in_specs=[smem, smem, smem, vmem, vmem],
        out_specs=[vmem, vmem],
        out_shape=[
            jax.ShapeDtypeStruct((source.shape[0] * PAGE, HEAD), BF16),
            jax.ShapeDtypeStruct((shards, returned_pages * PAGE, HEAD), BF16),
        ],
        compiler_params=params(16),
        cost_estimate=pl.CostEstimate(
            flops=4000000000, bytes_accessed=3000000, transcendentals=0
        ),
        name="blend",
    )(me, source, place, listed_lanes, received)


def turn_kernel(me_ref, mine, other, keys, values_t, longest, values, sems):
    length = keys.shape[0]
    core = me_ref[0] % 2

    @pl.when(core == 0)
    def _():
        pltpu.make_async_copy(mine, keys, sems.at[0]).start()
        pltpu.make_async_copy(other, values, sems.at[1]).start()

    @pl.when(core != 0)
    def _():
        pltpu.make_async_copy(other, keys, sems.at[0]).start()
        pltpu.make_async_copy(mine, values, sems.at[1]).start()

    pltpu.make_async_copy(mine, keys, sems.at[0]).wait()
    pltpu.make_async_copy(mine, values, sems.at[1]).wait()
    values_t[HEAD:, :] = jnp.ones((values_t.shape[0] - HEAD, length), BF16)
    ones = jnp.ones((HEAD, HEAD), BF16)
    most = jnp.zeros((8, HEAD), F32)
    for part in range(length // TURN):
        span = slice(part * TURN, (part + 1) * TURN)
        values_t[:HEAD, span] = values[span].T
        key = keys[span].astype(F32)
        squares = jnp.dot((key * key).astype(BF16), ones, preferred_element_type=F32)
        most = jnp.maximum(most, jnp.max(squares.reshape(TURN // 8, 8, HEAD), axis=0))
    longest[...] = jnp.broadcast_to(jnp.max(most, axis=0, keepdims=True), (8, HEAD))


def turn(me, mine, other):
    length = mine.shape[0]
    vmem = pl.BlockSpec(memory_space=VMEM)
    anywhere = pl.BlockSpec(memory_space=pl.ANY)
    return pl.pallas_call(
        turn_kernel,
        in_specs=[pl.BlockSpec(memory_space=SMEM), anywhere, anywhere],
        out_specs=[vmem, vmem, vmem],
        out_shape=[
            jax.ShapeDtypeStruct((length, HEAD), BF16),
            jax.ShapeDtypeStruct((HEAD + 16, length), BF16),
            jax.ShapeDtypeStruct((8, HEAD), F32),
        ],
        scratch_shapes=[pltpu.VMEM((length, HEAD), BF16), pltpu.SemaphoreType.DMA((2,))],
        compiler_params=params(16),
        cost_estimate=pl.CostEstimate(
            flops=100000000, bytes_accessed=3000000, transcendentals=0
        ),
        name="turn",
    )(me, mine, other)


SLACK = 60.0
LEAST = 2.0**-90


def attend_kernel(
    tiles, block_count, positions, longest, received, keys, values_t, out, scores, block
):
    length = keys.shape[0]
    shards = out.shape[0]
    rows = out.shape[1] // 2
    per_shard = rows // 16
    tokens = length // shards
    half = TILES * 16
    wide = 2 * half
    out[...] = jnp.zeros_like(out)

    def block_step(b, carry):
        first_tile = b * TILES
        for t in range(TILES):
            tile = tiles[first_tile + t]
            shard = tile // per_shard
            row = pl.multiple_of((tile - shard * per_shard) * 16, 16)
            block[t * 16 : (t + 1) * 16] = received[shard, pl.ds(row, 16), :]
            block[half + t * 16 : half + (t + 1) * 16] = received[shard, pl.ds(rows + row, 16), :]
        open_keys = (tiles[first_tile] // per_shard) * tokens
        seen_keys = (tiles[first_tile + TILES - 1] // per_shard + 1) * tokens
        open_chunks = open_keys // CHUNK
        seen_chunks = (seen_keys + CHUNK - 1) // CHUNK
        query = block[...]
        position = positions[b][:1]

        def score(chunk):
            start = pl.multiple_of(chunk * CHUNK, CHUNK)
            products = lax.dot_general(
                keys[pl.ds(start, CHUNK), :],
                query,
                (((1,), (1,)), ((), ())),
                preferred_element_type=F32,
            )
            return products * EXP2_SCALE

        def edge_score(chunk):
            found = score(chunk)
            key_position = chunk * CHUNK + lax.broadcasted_iota(I32, (CHUNK, wide), 0)
            return jnp.where(key_position <= position, found, MASKED)

        def add(chunk, found, shift, state):
            start = pl.multiple_of(chunk * CHUNK, CHUNK)
            exps = jnp.exp2(found - shift).astype(BF16)
            return state + jnp.dot(
                values_t[:, pl.ds(start, CHUNK)], exps, preferred_element_type=F32
            )

        def finish(state):
            total = state[HEAD : HEAD + 1]
            result = state[:HEAD] / jnp.where(total > 0, total, 1.0)
            result = jnp.where(position >= 0, result, 0.0).T.astype(BF16)
            for t in range(TILES):
                tile = tiles[first_tile + t]
                shard = tile // per_shard
                row = pl.multiple_of((tile - shard * per_shard) * 16, 16)
                out[shard, pl.ds(row, 16), :] = result[t * 16 : (t + 1) * 16]
                out[shard, pl.ds(rows + row, 16), :] = result[half + t * 16 : half + (t + 1) * 16]
            return total

        nothing = jnp.zeros((values_t.shape[0], wide), F32)
        squares = query.astype(F32)
        squares = lax.dot_general(
            jnp.ones((8, HEAD), BF16),
            (squares * squares).astype(BF16),
            (((1,), (1,)), ((), ())),
            preferred_element_type=F32,
        )
        bound = jnp.sqrt(squares[:1] * longest[:1, :1]) * (1.02 * EXP2_SCALE) - SLACK
        state = lax.fori_loop(
            0, open_chunks, lambda c, st: add(c, score(c), bound, st), nothing
        )
        state = lax.fori_loop(
            open_chunks, seen_chunks, lambda c, st: add(c, edge_score(c), bound, st), state
        )
        total = finish(state)
        lowest = jnp.min(jnp.where(position >= 0, total, 1.0))

        @pl.when(lowest < LEAST)
        def _():
            def keep(chunk, best):
                found = edge_score(chunk)
                scores[chunk] = found
                return jnp.maximum(best, jnp.max(found.reshape(CHUNK // 8, 8, wide), axis=0))

            best = lax.fori_loop(0, seen_chunks, keep, jnp.full((8, wide), MASKED, F32))
            best = jnp.max(best, axis=0, keepdims=True)
            finish(
                lax.fori_loop(
                    0, seen_chunks, lambda c, st: add(c, scores[c], best, st), nothing
                )
            )

        return carry

    lax.fori_loop(0, block_count[0], block_step, 0)


def attend(tiles, block_count, positions, longest, received, keys, values_t, rows):
    length = keys.shape[0]
    smem = pl.BlockSpec(memory_space=SMEM)
    vmem = pl.BlockSpec(memory_space=VMEM)
    block = 2 * TILES * 16
    return pl.pallas_call(
        attend_kernel,
        in_specs=[smem, smem, vmem, vmem, vmem, vmem, vmem],
        out_specs=vmem,
        out_shape=jax.ShapeDtypeStruct((received.shape[0], 2 * rows, HEAD), BF16),
        scratch_shapes=[
            pltpu.VMEM((length // CHUNK, CHUNK, block), F32),
            pltpu.VMEM((block, HEAD), BF16),
        ],
        compiler_params=params(28),
        cost_estimate=pl.CostEstimate(
            flops=16000000000, bytes_accessed=3000000, transcendentals=0
        ),
        name="attend",
    )(tiles, block_count, positions, longest, received, keys, values_t)


def place_cache_kernel(received, keys, values):
    own_pages, page_tokens, _ = keys.shape
    shared = received.shape[1] // page_tokens
    for part, target in ((0, keys), (1, values)):
        for page in range(own_pages):
            source, at = (part, page) if page < shared else (2 + part, page - own_pages + shared)
            target[page] = received[source, at * page_tokens : (at + 1) * page_tokens]


def place_cache(received, own_pages, page_tokens):
    shards, sent, _ = received.shape
    group = shards // KV_HEADS
    cache = jax.ShapeDtypeStruct((own_pages, page_tokens, KV_HEADS * HEAD), BF16)
    spec = pl.BlockSpec((own_pages, page_tokens, HEAD), lambda h: (0, 0, h))
    return pl.pallas_call(
        place_cache_kernel,
        grid=(KV_HEADS,),
        in_specs=[pl.BlockSpec((group, sent, HEAD), lambda h: (h, 0, 0))],
        out_specs=[spec, spec],
        out_shape=[cache, cache],
        compiler_params=params(16),
        cost_estimate=pl.CostEstimate(
            flops=2500000000, bytes_accessed=3000000, transcendentals=0
        ),
        name="place_cache",
    )(received)


def place_attended_kernel(received, out):
    rows = out.shape[0]
    for j in range(received.shape[0]):
        for t in range(2):
            head = 2 * j + t
            out[:, head * HEAD : (head + 1) * HEAD] = received[j, t * rows : (t + 1) * rows]


def place_attended(received):
    shards, sent, _ = received.shape
    steps = 4
    rows, width = sent // 2, shards * 2 * HEAD
    return pl.pallas_call(
        place_attended_kernel,
        grid=(steps,),
        in_specs=[pl.BlockSpec((shards // steps, sent, HEAD), lambda h: (h, 0, 0))],
        out_specs=pl.BlockSpec((rows, width // steps), lambda h: (0, h)),
        out_shape=jax.ShapeDtypeStruct((rows, width), BF16),
        compiler_params=params(16),
        cost_estimate=pl.CostEstimate(flops=0, bytes_accessed=1600000, transcendentals=0),
        name="place_attended",
    )(received)


def exchange(blocks):
    return lax.all_to_all(blocks, "shard", 0, 0)


def shard_program(
    shards,
    paged_key_store,
    paged_value_store,
    paged_scale_store,
    page_map,
    span_order,
    listed_count,
    listed_index,
    listed_queries,
    selected_token_keys,
    selected_token_values,
):
    own_pages, page_tokens, _ = paged_key_store.shape
    rows = listed_queries.shape[0]
    me = lax.axis_index("shard").astype(I32).reshape(1)

    received = exchange(
        prepare(
            me,
            page_map,
            span_order,
            listed_index,
            paged_scale_store.transpose(1, 2, 0),
            listed_queries,
            paged_key_store,
            paged_value_store,
            selected_token_keys,
            selected_token_values,
            shards,
        )
    )

    listed = jnp.arange(rows, dtype=I32)[None, :] < listed_count[:, None]
    listed_lanes = jnp.where(listed, listed_index.reshape(shards, rows), -1)
    source, place, tiles, block_count, positions = plan(
        page_map, span_order, listed_count, listed_lanes
    )

    mine, returned = blend(me, source, place, listed_lanes, received)
    other = lax.ppermute(mine, "shard", [(i, i ^ 1) for i in range(shards)])
    received_cache = exchange(returned)
    keys, values_t, longest = turn(me, mine, other)
    attended = attend(tiles, block_count, positions, longest, received, keys, values_t, rows)
    mixed_keys, mixed_values = place_cache(received_cache, own_pages, page_tokens)
    return mixed_keys, mixed_values, place_attended(exchange(attended))


def solution(mesh):
    split = ("req", "shard")
    in_specs = (
        P(split, None, None),
        P(split, None, None),
        P(split, None, None),
        P("req"),
        P("req"),
        P("req"),
        P("req"),
        P(split, None),
        P(split, None),
        P(split, None),
    )
    out_specs = (P(split, None, None), P(split, None, None), P(split, None))
    return jax.shard_map(
        functools.partial(shard_program, mesh.shape["shard"]),
        mesh=mesh,
        in_specs=in_specs,
        out_specs=out_specs,
        check_vma=False,
    )
```

time: 142 us -> 122 us (0.86); the launches traced: 140 us -> 122 us
  blocking collectives: 17.2 us -> 0 us
  local copies, waits for them, and re-layouts: 14.1 us -> 1.87 us
  waiting for transfers between devices: 25.9 us -> 36.9 us
    all_to_all x1 -> x0, blocking collectives: 17.2 us -> none  [exchange(): return lax.all_to_all(blocks, 'shard', 0, 0)]
    unnamed x37 -> x12, local copies, waits for them, and re-layouts: 13.9 us -> 1.79 us
    all_to_all x3, waiting for transfers between devices: 25.9 us -> 36.9 us  [exchange(): return lax.all_to_all(blocks, 'shard', 0, 0)]
    pallas_call x3, Pallas kernels: 40.6 us -> 45.1 us  [the longest x1 35 us: attend(): pl.pallas_call(attend_kernel, in_specs=[smem, smem, vmem, vmem, vmem, vme...]
    pallas_call x1, Pallas kernels: 7.67 us -> 3.88 us  [blend(): pl.pallas_call(blend_kernel, in_specs=[smem, smem, smem, vmem, vmem], out...]
  transfers between devices with their start and end apart: 4 -> 4, of which waited for: 2 -> 2; matrix products, arithmetic and copies ran while one was open for 0% -> 0% of each run, Pallas kernels for 34% -> 40%
where the time goes in v2:
time: 122 us
  Pallas kernels  61.5 us (50%)
  waiting for transfers between devices  36.9 us (30%)
  starting transfers between devices  20.8 us (17%)
  local copies, waits for them, and re-layouts  1.87 us (2%)
    all_to_all x3, waiting for transfers between devices, exchange(): return lax.all_to_all(blocks, 'shard', 0, 0)  36.9 us
    pallas_call x1, Pallas kernels, attend(): pl.pallas_call(attend_kernel, in_specs=[smem, smem, vmem, vmem, vmem, vme...  35 us
    all_to_all x3, starting transfers between devices, exchange(): return lax.all_to_all(blocks, 'shard', 0, 0)  19.8 us
    pallas_call x1, Pallas kernels, plan(): pl.pallas_call(plan_kernel, in_specs=[smem, smem, smem, vmem], out_specs=...  8.43 us
    pallas_call x1, Pallas kernels, prepare(): pl.pallas_call(prepare_kernel, grid=(KV_HEADS,), in_specs=[smem, smem, sm...  7.51 us
    pallas_call x1, Pallas kernels, blend(): pl.pallas_call(blend_kernel, in_specs=[smem, smem, smem, vmem, vmem], out...  3.88 us
    pallas_call x1, Pallas kernels, place_cache(): pl.pallas_call(place_cache_kernel, grid=(KV_HEADS,), in_specs=[pl.BlockSp...  2.62 us
    pallas_call x1, Pallas kernels, turn(): pl.pallas_call(turn_kernel, in_specs=[pl.BlockSpec(memory_space=SMEM), an...  2.6 us
  transfers between devices with their start and end apart: 4, of which 2 were waited for; matrix products, arithmetic and copies ran while one was open for 0% of the time, Pallas kernels for 40%

profile of v2, /device:TPU:1, one launch (start us, length us, event | category | flops | bytes accessed | tf_op | source)
XLA Modules:
  0.0 121.8 jit_solution(14238396325918196709)
XLA Ops:
  0.6 7.5 %prepare.1 = bf16[32,320,128]{2,1,0:T(8,128)(2,1)} custom-call(s32[1]{0:T(128)} %bitcast.me_ref, s32[352]{0:T(512)} %page_map.3, s32[8]{0:T(128)} %span_order.3, s32[1536]{0:T(1024)} %listed_index.1, f32[2,8,11]{2,1,0:T(8,128)} %bitcast.2, f32[1,128]{1,0:T(1,128)} %constant.8.clone.frequency, bf16[48,8192]{1,0:T(8,128)(2,1)} %queries.1, ...), custom_call_target="tpu_custom_call" | custom-call | flops 5000000000 | bytes 4300000 | tf_op jit(solution)/shard_map/prepare/pallas_call | solution.py:142
  8.1 0.0 copy-start.5
  8.2 0.0 copy-start.2
  8.2 0.0 copy-start.3
  8.2 0.0 copy-start.4
  8.2 8.7 %all-to-all-start = ((bf16[32,320,128]{2,1,0:T(8,128)(2,1)}), bf16[32,320,128]{2,1,0:T(8,128)(2,1)S(1)}, u32[]{:S(2)}, u32[]{:S(2)}) async-start(bf16[32,320,128]{2,1,0:T(8,128)(2,1)} %prepare.1), calls=%async_computation | async-start | bytes 5242880 | tf_op jit(solution)/shard_map/all_to_all | solution.py:584
  16.9 0.0 copy-done.5
  16.9 0.1 reshape.14
  17.0 0.0 copy-done.2
  17.0 0.1 fusion.listed_lanes
  17.1 0.0 copy-done.3
  17.1 0.0 copy-done.4
  17.1 8.4 %plan.1 = (s32[352]{0:T(512)S(1)}, s32[352]{0:T(512)S(1)}, s32[112]{0:T(128)S(1)}, s32[1]{0:T(128)}, s32[6,8,512]{2,1,0:T(8,128)S(1)}) custom-call(s32[352]{0:T(512)S(1)} %copy-done.3, s32[8]{0:T(128)S(1)} %copy-done.4, s32[32]{0:T(128)S(1)} %copy-done.2, s32[32,48]{1,0:T(8,128)S(1)} %fusion.listed_lanes), custom_call_target="tpu_custom_call" | custom-call | flops 8999999488 | bytes 3000000 | tf_op jit(solution)/shard_map/plan/pallas_call | solution.py:275
  25.5 25.3 %all-to-all-done.received = bf16[32,320,128]{2,1,0:T(8,128)(2,1)S(1)} async-done(((bf16[32,320,128]{2,1,0:T(8,128)(2,1)}), bf16[32,320,128]{2,1,0:T(8,128)(2,1)S(1)}, u32[]{:S(2)}, u32[]{:S(2)}) %all-to-all-start) | async-done | bytes 2621472 | tf_op jit(solution)/shard_map/all_to_all | solution.py:584
  50.8 3.9 %blend.1 = (bf16[5632,128]{1,0:T(8,128)(2,1)}, bf16[32,96,128]{2,1,0:T(8,128)(2,1)S(1)}) custom-call(s32[1]{0:T(128)} %bitcast.me_ref, s32[352]{0:T(512)S(1)} %get-tuple-element.15.source, s32[352]{0:T(512)S(1)} %get-tuple-element.16.place, s32[32,48]{1,0:T(8,128)S(1)} %fusion.listed_lanes, bf16[32,320,128]{2,1,0:T(8,128)(2,1)S(1)} %all-to-all-done.received), custom_call_target="tpu_custom_call" | custom-call | flops 4000000000 | bytes 3000000 | tf_op jit(solution)/shard_map/blend/pallas_call | solution.py:340
  54.7 0.0 copy-start
  54.7 0.9 copy-done
  55.6 1.0 collective-permute-start
  56.5 3.7 %all-to-all-start.1 = ((bf16[32,96,128]{2,1,0:T(8,128)(2,1)}), bf16[32,96,128]{2,1,0:T(8,128)(2,1)S(1)}, u32[]{:S(2)}, u32[]{:S(2)}) async-start(bf16[32,96,128]{2,1,0:T(8,128)(2,1)} %copy-done), calls=%async_computation.1 | async-start | bytes 1572864 | tf_op jit(solution)/shard_map/all_to_all | solution.py:584
  60.3 0.0 collective-permute-done.other
  60.3 2.6 %turn.1 = (bf16[5632,128]{1,0:T(8,128)(2,1)S(1)}, bf16[144,5632]{1,0:T(8,128)(2,1)S(1)}, f32[8,128]{1,0:T(8,128)S(1)}) custom-call(s32[1]{0:T(128)} %bitcast.me_ref, bf16[5632,128]{1,0:T(8,128)(2,1)} %get-tuple-element.23.mine, bf16[5632,128]{1,0:T(8,128)(2,1)} %collective-permute-done.other), custom_call_target="tpu_custom_call" | custom-call | flops 100000000 | bytes 3000000 | tf_op jit(solution)/shard_map/turn/pallas_call | solution.py:388
  62.9 35.0 %attend.1 = bf16[32,96,128]{2,1,0:T(8,128)(2,1)S(1)} custom-call(s32[112]{0:T(128)S(1)} %get-tuple-element.20.tiles, s32[1]{0:T(128)} %get-tuple-element.21.block_count, s32[6,8,512]{2,1,0:T(8,128)S(1)} %get-tuple-element.22.positions, f32[8,128]{1,0:T(8,128)S(1)} %get-tuple-element.24.longest, bf16[32,320,128]{2,1,0:T(8,128)(2,1)S(1)} %all-to-all-done.received, ...), custom_call_target="tpu_custom_call" | custom-call | flops 16000000000 | bytes 3000000 | tf_op jit(solution)/shard_map/attend/pallas_call | solution.py:514
  97.8 0.0 copy-start.1
  97.8 0.9 copy-done.1
  98.7 0.0 all-to-all-done.1.received
  98.7 7.4 %all-to-all-start.2 = ((bf16[32,96,128]{2,1,0:T(8,128)(2,1)}), bf16[32,96,128]{2,1,0:T(8,128)(2,1)S(1)}, u32[]{:S(2)}, u32[]{:S(2)}) async-start(bf16[32,96,128]{2,1,0:T(8,128)(2,1)} %copy-done.1), calls=%async_computation.2 | async-start | bytes 1572864 | tf_op jit(solution)/shard_map/all_to_all | solution.py:584
  106.1 2.6 %place_cache.1 = (bf16[11,16,1024]{2,1,0:T(8,128)(2,1)}, bf16[11,16,1024]{2,1,0:T(8,128)(2,1)}) custom-call(bf16[32,96,128]{2,1,0:T(8,128)(2,1)S(1)} %all-to-all-done.1.received), custom_call_target="tpu_custom_call" | custom-call | flops 2500000000 | bytes 3000000 | tf_op jit(solution)/shard_map/place_cache/pallas_call | solution.py:545
  108.7 11.6 %all-to-all-done.2.received = bf16[32,96,128]{2,1,0:T(8,128)(2,1)S(1)} async-done(((bf16[32,96,128]{2,1,0:T(8,128)(2,1)}), bf16[32,96,128]{2,1,0:T(8,128)(2,1)S(1)}, u32[]{:S(2)}, u32[]{:S(2)}) %all-to-all-start.2) | async-done | bytes 786464 | tf_op jit(solution)/shard_map/all_to_all | solution.py:584
  120.3 1.5 %place_attended.1 = bf16[48,8192]{1,0:T(8,128)(2,1)} custom-call(bf16[32,96,128]{2,1,0:T(8,128)(2,1)S(1)} %all-to-all-done.2.received), custom_call_target="tpu_custom_call" | custom-call | bytes 1600000 | tf_op jit(solution)/shard_map/place_attended/pallas_call | solution.py:571
Async XLA Ops:
  8.1 8.8 %copy-start.5 = (s32[1536]{0:T(1024)S(1)}, s32[1536]{0:T(1024)}, u32[]{:S(2)}) copy-start(s32[1536]{0:T(1024)} %listed_index.1) | copy-start | bytes 18436
  8.2 8.9 %copy-start.2 = (s32[32]{0:T(128)S(1)}, s32[32]{0:T(128)}, u32[]{:S(2)}) copy-start(s32[32]{0:T(128)} %listed_count.1) | copy-start | bytes 388
  8.2 8.9 %copy-start.3 = (s32[352]{0:T(512)S(1)}, s32[352]{0:T(512)}, u32[]{:S(2)}) copy-start(s32[352]{0:T(512)} %page_map.3) | copy-start | bytes 4228
  8.2 8.9 %copy-start.4 = (s32[8]{0:T(128)S(1)}, s32[8]{0:T(128)}, u32[]{:S(2)}) copy-start(s32[8]{0:T(128)} %span_order.3) | copy-start | bytes 100
  8.2 42.6 %all-to-all-start = ((bf16[32,320,128]{2,1,0:T(8,128)(2,1)}), bf16[32,320,128]{2,1,0:T(8,128)(2,1)S(1)}, u32[]{:S(2)}, u32[]{:S(2)}) async-start(bf16[32,320,128]{2,1,0:T(8,128)(2,1)} %prepare.1), calls=%async_computation | async-start | bytes 5242880 | tf_op jit(solution)/shard_map/all_to_all | solution.py:584
  54.7 0.9 copy-start
  55.6 4.7 %collective-permute-start = (bf16[5632,128]{1,0:T(8,128)(2,1)}, bf16[5632,128]{1,0:T(8,128)(2,1)}, u32[]{:S(2)}, u32[]{:S(2)}) collective-permute-start(bf16[5632,128]{1,0:T(8,128)(2,1)} %get-tuple-element.23.mine), channel_id=1, source_target_pairs={{0,1},{1,0},{2,3},{3,2},{4,5},{5,4},{6,7},{7,6},{8,9},{9,8},{10,11... | collective-permute-start | bytes 4325384 | tf_op jit(solution)/shard_map/ppermute | solution.py:627
  56.5 42.2 %all-to-all-start.1 = ((bf16[32,96,128]{2,1,0:T(8,128)(2,1)}), bf16[32,96,128]{2,1,0:T(8,128)(2,1)S(1)}, u32[]{:S(2)}, u32[]{:S(2)}) async-start(bf16[32,96,128]{2,1,0:T(8,128)(2,1)} %copy-done), calls=%async_computation.1 | async-start | bytes 1572864 | tf_op jit(solution)/shard_map/all_to_all | solution.py:584
  97.8 0.9 copy-start.1
  98.7 21.6 %all-to-all-start.2 = ((bf16[32,96,128]{2,1,0:T(8,128)(2,1)}), bf16[32,96,128]{2,1,0:T(8,128)(2,1)S(1)}, u32[]{:S(2)}, u32[]{:S(2)}) async-start(bf16[32,96,128]{2,1,0:T(8,128)(2,1)} %copy-done.1), calls=%async_computation.2 | async-start | bytes 1572864 | tf_op jit(solution)/shard_map/all_to_all | solution.py:584

commit v3 on v2

--- a/solution.py
+++ b/solution.py
@@ -16,8 +16,10 @@
 VMEM_MIB = 56
 TILES = 16
 CHUNK = 1408
-TURN = 512
 PAGE = 16
+BIG = 22
+MID = 11
+SMALL = 4
 EXP2_SCALE = float(HEAD**-0.5 / np.log(2.0))
 
 BF16 = jnp.bfloat16
@@ -25,6 +27,7 @@
 I32 = jnp.int32
 SMEM = pltpu.SMEM
 VMEM = pltpu.VMEM
+OUT_SPACE = pltpu.HBM
 
 
 def rope_frequency():
@@ -55,69 +58,98 @@
     listed_index,
     scale,
     frequency,
+    queries_in,
+    keys_in,
+    values_in,
+    fresh_keys_in,
+    fresh_values_in,
+    out,
     queries,
     keys,
     values,
     fresh_keys,
     fresh_values,
-    out,
+    blocks,
     slots,
     positions,
-    row_cos,
-    row_sin,
     shift_cos,
     shift_sin,
+    in_sems,
+    out_sems,
 ):
-    head = pl.program_id(0)
     me = me_ref[0]
     own_pages, page_tokens, _ = keys.shape
     rows = fresh_keys.shape[0]
-    group = out.shape[0]
+    group = blocks.shape[0] // KV_HEADS
     span_count = span_order.shape[0]
     per_span = page_map.shape[0] // span_count
     tokens = own_pages * page_tokens
-
-    @pl.when(head == 0)
-    def _():
-        first = me * own_pages
-        for slot in range(span_count):
-            start = span_order[slot] * per_span
-
-            def note(p, carry):
-                place = page_map[start + p] - first
-                inside = (place >= 0) & (place < own_pages)
-                slots[jnp.where(inside, place, own_pages)] = slot
-                return carry
-
-            lax.fori_loop(0, per_span, note, 0, unroll=11)
-        for c in range(rows):
-            position = (me * tokens + listed_index[me * rows + c]).astype(F32)
-            positions[c : c + 1, :] = jnp.full((1, HEAD), position, F32)
-        row_cos[...], row_sin[...] = rope_tables(positions[...], frequency[...])
-        shift = lax.broadcasted_iota(I32, (span_count, HEAD), 0) * SPAN_LEN
-        shift_cos[...], shift_sin[...] = rope_tables(shift.astype(F32), frequency[...])
-
-    cosine, sine = row_cos[...], row_sin[...]
-    for j in range(group):
-        for t in range(2):
-            at = (2 * j + t) * HEAD
-            x = queries[:, at : at + HEAD].astype(F32)
-            out[j, t * rows : (t + 1) * rows] = rotate(x, cosine, sine).astype(BF16)
-    base = 2 * rows
-    for page in range(own_pages):
-        slot = slots[page]
-        page_cos = shift_cos[pl.ds(slot, 1), :]
-        page_sin = shift_sin[pl.ds(slot, 1), :]
-        span = slice(base + page * page_tokens, base + (page + 1) * page_tokens)
-        key = keys[page].astype(F32) * scale[0, head, page]
-        key = rotate(key, page_cos, page_sin).astype(BF16)
-        value = (values[page].astype(F32) * scale[1, head, page]).astype(BF16)
+    arrivals = [
+        pltpu.make_async_copy(source, target, in_sems.at[i])
+        for i, (source, target) in enumerate(
+            (
+                (queries_in, queries),
+                (keys_in, keys),
+                (values_in, values),
+                (fresh_keys_in, fresh_keys),
+                (fresh_values_in, fresh_values),
+            )
+        )
+    ]
+    for arrival in arrivals:
+        arrival.start()
+
+    for c in range(rows):
+        position = (me * tokens + listed_index[me * rows + c]).astype(F32)
+        positions[c : c + 1, :] = jnp.full((1, HEAD), position, F32)
+    cosine, sine = rope_tables(positions[...], frequency[...])
+    shift = lax.broadcasted_iota(I32, (span_count, HEAD), 0) * SPAN_LEN
+    shift_cos[...], shift_sin[...] = rope_tables(shift.astype(F32), frequency[...])
+    first = me * own_pages
+    for slot in range(span_count):
+        start = span_order[slot] * per_span
+
+        def note(p, carry):
+            place = page_map[start + p] - first
+            inside = (place >= 0) & (place < own_pages)
+            slots[jnp.where(inside, place, own_pages)] = slot
+            return carry
+
+        lax.fori_loop(0, per_span, note, 0, unroll=11)
+    page_slots = [slots[page] for page in range(own_pages)]
+    for arrival in arrivals:
+        arrival.wait()
+
+    departures = []
+    for head in range(KV_HEADS):
+        lanes = slice(head * HEAD, (head + 1) * HEAD)
+        outs = [head * group + j for j in range(group)]
         for j in range(group):
-            out[j, span] = value if j % 2 else key
-    key = rotate(fresh_keys[...].astype(F32), cosine, sine).astype(BF16)
-    value = fresh_values[...]
-    for j in range(group):
-        out[j, base + tokens :] = value if j % 2 else key
+            for t in range(2):
+                at = (2 * (head * group + j) + t) * HEAD
+                x = queries[:, at : at + HEAD].astype(F32)
+                blocks[outs[j], t * rows : (t + 1) * rows] = rotate(x, cosine, sine).astype(BF16)
+        base = 2 * rows
+        for page in range(own_pages):
+            page_cos = shift_cos[pl.ds(page_slots[page], 1), :]
+            page_sin = shift_sin[pl.ds(page_slots[page], 1), :]
+            span = slice(base + page * page_tokens, base + (page + 1) * page_tokens)
+            key = keys[page, :, lanes].astype(F32) * scale[0, head, page]
+            key = rotate(key, page_cos, page_sin).astype(BF16)
+            value = (values[page, :, lanes].astype(F32) * scale[1, head, page]).astype(BF16)
+            for j in range(group):
+                blocks[outs[j], span] = value if j % 2 else key
+        key = rotate(fresh_keys[:, lanes].astype(F32), cosine, sine).astype(BF16)
+        value = fresh_values[:, lanes]
+        for j in range(group):
+            blocks[outs[j], base + tokens :] = value if j % 2 else key
+        span = pl.ds(head * group, group)
+        departures.append(
+            pltpu.make_async_copy(blocks.at[span], out.at[span], out_sems.at[head])
+        )
+        departures[-1].start()
+    for departure in departures:
+        departure.wait()
 
 
 def prepare(
@@ -137,33 +169,23 @@
     rows, width = queries.shape
     sent = 3 * rows + own_pages * page_tokens
     smem = pl.BlockSpec(memory_space=SMEM)
-    pages = pl.BlockSpec((own_pages, page_tokens, HEAD), lambda h: (0, 0, h))
-    fresh = pl.BlockSpec((rows, HEAD), lambda h: (0, h))
+    vmem = pl.BlockSpec(memory_space=VMEM)
+    anywhere = pl.BlockSpec(memory_space=pl.ANY)
+    arrays = (queries, keys, values, fresh_keys, fresh_values)
     return pl.pallas_call(
         prepare_kernel,
-        grid=(KV_HEADS,),
-        in_specs=[
-            smem,
-            smem,
-            smem,
-            smem,
-            smem,
-            pl.BlockSpec((1, HEAD), lambda h: (0, 0)),
-            pl.BlockSpec((rows, width // KV_HEADS), lambda h: (0, h)),
-            pages,
-            pages,
-            fresh,
-            fresh,
-        ],
-        out_specs=pl.BlockSpec((shards // KV_HEADS, sent, HEAD), lambda h: (h, 0, 0)),
+        in_specs=[smem] * 5 + [vmem] + [anywhere] * 5,
+        out_specs=pl.BlockSpec(memory_space=OUT_SPACE),
         out_shape=jax.ShapeDtypeStruct((shards, sent, HEAD), BF16),
-        scratch_shapes=[
+        scratch_shapes=[pltpu.VMEM(a.shape, a.dtype) for a in arrays]
+        + [
+            pltpu.VMEM((shards, sent, HEAD), BF16),
             pltpu.SMEM((own_pages + 1,), I32),
-            pltpu.VMEM((rows, HEAD), F32),
-            pltpu.VMEM((rows, HEAD), F32),
             pltpu.VMEM((rows, HEAD), F32),
             pltpu.VMEM((span_order.shape[0], HEAD), F32),
             pltpu.VMEM((span_order.shape[0], HEAD), F32),
+            pltpu.SemaphoreType.DMA((len(arrays),)),
+            pltpu.SemaphoreType.DMA((KV_HEADS,)),
         ],
         compiler_params=params(VMEM_MIB),
         cost_estimate=pl.CostEstimate(
@@ -177,11 +199,7 @@
         listed_index,
         scale,
         jnp.asarray(rope_frequency()),
-        queries,
-        keys,
-        values,
-        fresh_keys,
-        fresh_values,
+        *arrays,
     )
 
 
@@ -292,31 +310,58 @@
     )(page_map, span_order, listed_count, listed_lanes)
 
 
-def blend_kernel(me_ref, source, place, listed_lanes, received, ordered, returned):
+GROUPS = 4
+
+
+def blend_kernel(
+    me_ref, source, place, listed_lanes, received, mine, returned, ordered, blocks, sems
+):
     shards, sent, _ = received.shape
     rows = listed_lanes.shape[1]
     own_pages = source.shape[0] // shards
     page_tokens = PAGE
     tokens = own_pages * page_tokens
+    part = shards // GROUPS
+    per_part = part * tokens // HEAD
+    is_key = me_ref[0] % 2 == 0
     flat = received.reshape(shards * sent, HEAD)
     token = lax.broadcasted_iota(I32, (tokens, rows), 0)
     ones = jnp.ones((rows, HEAD), BF16)
-
-    def shard_step(shard, carry):
-        pages = []
-        for page in range(own_pages):
-            start = pl.multiple_of(source[shard * own_pages + page], page_tokens)
-            pages.append(flat[pl.ds(start, page_tokens), :])
-        cached = jnp.concatenate(pages, axis=0)
-        pick = jnp.where(listed_lanes[pl.ds(shard, 1), :] == token, 1.0, 0.0).astype(BF16)
-        fresh = jnp.concatenate([received[shard, 2 * rows + tokens :, :], ones], axis=1)
-        found = jnp.dot(pick, fresh, preferred_element_type=F32)
-        mixed = jnp.where(found[:, HEAD:] > 0.5, found[:, :HEAD], cached.astype(F32))
-        start = pl.multiple_of(shard * tokens, 16)
-        ordered[pl.ds(start, tokens), :] = mixed.astype(BF16)
-        return carry
-
-    lax.fori_loop(0, shards, shard_step, 0, unroll=4)
+    all_ones = jnp.ones((HEAD, HEAD), BF16)
+
+    def send(g):
+        span = pl.ds(g * per_part, per_part)
+        return pltpu.make_async_copy(blocks.at[span], mine.at[span], sems.at[g])
+
+    def group_step(g, most):
+        for u in range(part):
+            shard = g * part + u
+            pages = []
+            for page in range(own_pages):
+                start = pl.multiple_of(source[shard * own_pages + page], page_tokens)
+                pages.append(flat[pl.ds(start, page_tokens), :])
+            cached = jnp.concatenate(pages, axis=0)
+            pick = jnp.where(listed_lanes[pl.ds(shard, 1), :] == token, 1.0, 0.0).astype(BF16)
+            fresh = jnp.concatenate([received[shard, 2 * rows + tokens :, :], ones], axis=1)
+            found = jnp.dot(pick, fresh, preferred_element_type=F32)
+            mixed = jnp.where(found[:, HEAD:] > 0.5, found[:, :HEAD], cached.astype(F32))
+            start = pl.multiple_of(shard * tokens, 16)
+            ordered[pl.ds(start, tokens), :] = mixed.astype(BF16)
+            squares = jnp.dot((mixed * mixed).astype(BF16), all_ones, preferred_element_type=F32)
+            most = jnp.maximum(most, jnp.max(squares.reshape(tokens // 8, 8, HEAD), axis=0))
+        for u in range(per_part):
+            at = g * per_part + u
+            block = ordered[pl.ds(pl.multiple_of(at * HEAD, HEAD), HEAD), :]
+            blocks[at] = jnp.where(is_key, block, block.T)
+        send(g).start()
+        return most
+
+    most = lax.fori_loop(0, GROUPS, group_step, jnp.zeros((8, HEAD), F32))
+    most = jnp.max(most, axis=0, keepdims=True)
+    last = GROUPS * per_part
+    blocks[last] = jnp.broadcast_to(most, (HEAD, HEAD)).astype(BF16)
+    send_last = pltpu.make_async_copy(blocks.at[last], mine.at[last], sems.at[GROUPS])
+    send_last.start()
 
     returned_pages = returned.shape[1] // page_tokens
     first = ((me_ref[0] // 2) % 2) * (own_pages - returned_pages)
@@ -329,21 +374,30 @@
         return carry
 
     lax.fori_loop(0, shards, return_step, 0, unroll=4)
+    for g in range(GROUPS):
+        send(g).wait()
+    send_last.wait()
 
 
 def blend(me, source, place, listed_lanes, received):
     shards, rows = listed_lanes.shape
-    own_pages = source.shape[0] // shards
-    returned_pages = (own_pages + 1) // 2
+    pages = source.shape[0]
+    returned_pages = (pages // shards + 1) // 2
     smem = pl.BlockSpec(memory_space=SMEM)
     vmem = pl.BlockSpec(memory_space=VMEM)
+    blocks = (pages * PAGE // HEAD + 1, HEAD, HEAD)
     return pl.pallas_call(
         blend_kernel,
         in_specs=[smem, smem, smem, vmem, vmem],
-        out_specs=[vmem, vmem],
+        out_specs=[pl.BlockSpec(memory_space=OUT_SPACE), vmem],
         out_shape=[
-            jax.ShapeDtypeStruct((source.shape[0] * PAGE, HEAD), BF16),
+            jax.ShapeDtypeStruct(blocks, BF16),
             jax.ShapeDtypeStruct((shards, returned_pages * PAGE, HEAD), BF16),
+        ],
+        scratch_shapes=[
+            pltpu.VMEM((pages * PAGE, HEAD), BF16),
+            pltpu.VMEM(blocks, BF16),
+            pltpu.SemaphoreType.DMA((GROUPS + 1,)),
         ],
         compiler_params=params(16),
         cost_estimate=pl.CostEstimate(
@@ -353,71 +407,38 @@
     )(me, source, place, listed_lanes, received)
 
 
-def turn_kernel(me_ref, mine, other, keys, values_t, longest, values, sems):
-    length = keys.shape[0]
+SLACK = 60.0
+LEAST = 2.0**-90
+
+
+def attend_kernel(
+    me_ref, tiles, block_count, positions, received, mine, other, out, scores, block
+):
     core = me_ref[0] % 2
+    out[...] = jnp.zeros_like(out)
 
     @pl.when(core == 0)
     def _():
-        pltpu.make_async_copy(mine, keys, sems.at[0]).start()
-        pltpu.make_async_copy(other, values, sems.at[1]).start()
+        attend_blocks(tiles, block_count, positions, received, mine, other, out, scores, block)
 
     @pl.when(core != 0)
     def _():
-        pltpu.make_async_copy(other, keys, sems.at[0]).start()
-        pltpu.make_async_copy(mine, values, sems.at[1]).start()
-
-    pltpu.make_async_copy(mine, keys, sems.at[0]).wait()
-    pltpu.make_async_copy(mine, values, sems.at[1]).wait()
-    values_t[HEAD:, :] = jnp.ones((values_t.shape[0] - HEAD, length), BF16)
-    ones = jnp.ones((HEAD, HEAD), BF16)
-    most = jnp.zeros((8, HEAD), F32)
-    for part in range(length // TURN):
-        span = slice(part * TURN, (part + 1) * TURN)
-        values_t[:HEAD, span] = values[span].T
-        key = keys[span].astype(F32)
-        squares = jnp.dot((key * key).astype(BF16), ones, preferred_element_type=F32)
-        most = jnp.maximum(most, jnp.max(squares.reshape(TURN // 8, 8, HEAD), axis=0))
-    longest[...] = jnp.broadcast_to(jnp.max(most, axis=0, keepdims=True), (8, HEAD))
-
-
-def turn(me, mine, other):
-    length = mine.shape[0]
-    vmem = pl.BlockSpec(memory_space=VMEM)
-    anywhere = pl.BlockSpec(memory_space=pl.ANY)
-    return pl.pallas_call(
-        turn_kernel,
-        in_specs=[pl.BlockSpec(memory_space=SMEM), anywhere, anywhere],
-        out_specs=[vmem, vmem, vmem],
-        out_shape=[
-            jax.ShapeDtypeStruct((length, HEAD), BF16),
-            jax.ShapeDtypeStruct((HEAD + 16, length), BF16),
-            jax.ShapeDtypeStruct((8, HEAD), F32),
-        ],
-        scratch_shapes=[pltpu.VMEM((length, HEAD), BF16), pltpu.SemaphoreType.DMA((2,))],
-        compiler_params=params(16),
-        cost_estimate=pl.CostEstimate(
-            flops=100000000, bytes_accessed=3000000, transcendentals=0
-        ),
-        name="turn",
-    )(me, mine, other)
-
-
-SLACK = 60.0
-LEAST = 2.0**-90
-
-
-def attend_kernel(
-    tiles, block_count, positions, longest, received, keys, values_t, out, scores, block
+        attend_blocks(tiles, block_count, positions, received, other, mine, out, scores, block)
+
+
+def attend_blocks(
+    tiles, block_count, positions, received, keys, values_t, out, scores, block
 ):
-    length = keys.shape[0]
+    chunks = scores.shape[0]
+    per_chunk = CHUNK // HEAD
     shards = out.shape[0]
     rows = out.shape[1] // 2
     per_shard = rows // 16
-    tokens = length // shards
+    tokens = chunks * CHUNK // shards
     half = TILES * 16
     wide = 2 * half
-    out[...] = jnp.zeros_like(out)
+    top = keys[chunks * per_chunk, :1, :1].astype(F32)
+    ones = jnp.ones((16, max(BIG, per_chunk) * HEAD), BF16)
 
     def block_step(b, carry):
         first_tile = b * TILES
@@ -429,32 +450,29 @@
             block[half + t * 16 : half + (t + 1) * 16] = received[shard, pl.ds(rows + row, 16), :]
         open_keys = (tiles[first_tile] // per_shard) * tokens
         seen_keys = (tiles[first_tile + TILES - 1] // per_shard + 1) * tokens
-        open_chunks = open_keys // CHUNK
         seen_chunks = (seen_keys + CHUNK - 1) // CHUNK
         query = block[...]
         position = positions[b][:1]
 
-        def score(chunk):
-            start = pl.multiple_of(chunk * CHUNK, CHUNK)
+        def score(start, count):
             products = lax.dot_general(
-                keys[pl.ds(start, CHUNK), :],
+                keys[pl.ds(start, count)].reshape(count * HEAD, HEAD),
                 query,
                 (((1,), (1,)), ((), ())),
                 preferred_element_type=F32,
             )
             return products * EXP2_SCALE
 
-        def edge_score(chunk):
-            found = score(chunk)
-            key_position = chunk * CHUNK + lax.broadcasted_iota(I32, (CHUNK, wide), 0)
+        def edge_score(start, count):
+            found = score(start, count)
+            key_position = start * HEAD + lax.broadcasted_iota(I32, (count * HEAD, wide), 0)
             return jnp.where(key_position <= position, found, MASKED)
 
-        def add(chunk, found, shift, state):
-            start = pl.multiple_of(chunk * CHUNK, CHUNK)
+        def add(start, count, found, shift, state):
             exps = jnp.exp2(found - shift).astype(BF16)
-            return state + jnp.dot(
-                values_t[:, pl.ds(start, CHUNK)], exps, preferred_element_type=F32
-            )
+            value = [values_t[start + u] for u in range(count)]
+            value = jnp.concatenate([jnp.concatenate(value, axis=1), ones[:, : count * HEAD]], axis=0)
+            return state + jnp.dot(value, exps, preferred_element_type=F32)
 
         def finish(state):
             total = state[HEAD : HEAD + 1]
@@ -464,11 +482,13 @@
                 tile = tiles[first_tile + t]
                 shard = tile // per_shard
                 row = pl.multiple_of((tile - shard * per_shard) * 16, 16)
-                out[shard, pl.ds(row, 16), :] = result[t * 16 : (t + 1) * 16]
-                out[shard, pl.ds(rows + row, 16), :] = result[half + t * 16 : half + (t + 1) * 16]
+                low = result[t * 16 : (t + 1) * 16]
+                high = result[half + t * 16 : half + (t + 1) * 16]
+                out[shard, pl.ds(row, 16), :] = low
+                out[shard, pl.ds(rows + row, 16), :] = high
             return total
 
-        nothing = jnp.zeros((values_t.shape[0], wide), F32)
+        nothing = jnp.zeros((HEAD + 16, wide), F32)
         squares = query.astype(F32)
         squares = lax.dot_general(
             jnp.ones((8, HEAD), BF16),
@@ -476,12 +496,33 @@
             (((1,), (1,)), ((), ())),
             preferred_element_type=F32,
         )
-        bound = jnp.sqrt(squares[:1] * longest[:1, :1]) * (1.02 * EXP2_SCALE) - SLACK
+        bound = jnp.sqrt(squares[:1] * top) * (1.02 * EXP2_SCALE) - SLACK
+        seen = seen_keys // PAGE
+        big, mid, small = BIG * HEAD // PAGE, MID * HEAD // PAGE, SMALL * HEAD // PAGE
+        big_steps = seen // big
+        rest = seen - big_steps * big
+        big_steps = big_steps + jnp.where(rest > mid + small, 1, 0)
+        rest = jnp.where(rest > mid + small, 0, rest)
+        mid_steps = jnp.where(rest > small, 1, 0)
+        small_steps = jnp.where(rest > mid_steps * mid, 1, 0)
+        open_steps = open_keys // (BIG * HEAD)
+        mid_from = big_steps * BIG
+        small_from = mid_from + mid_steps * MID
+
+        def open_step(c, st):
+            start = c * BIG
+            return add(start, BIG, score(start, BIG), bound, st)
+
+        def edge_step(start, count, st):
+            return add(start, count, edge_score(start, count), bound, st)
+
+        state = lax.fori_loop(0, open_steps, open_step, nothing)
         state = lax.fori_loop(
-            0, open_chunks, lambda c, st: add(c, score(c), bound, st), nothing
+            open_steps, big_steps, lambda c, st: edge_step(c * BIG, BIG, st), state
         )
+        state = lax.fori_loop(0, mid_steps, lambda c, st: edge_step(mid_from, MID, st), state)
         state = lax.fori_loop(
-            open_chunks, seen_chunks, lambda c, st: add(c, edge_score(c), bound, st), state
+            0, small_steps, lambda c, st: edge_step(small_from, SMALL, st), state
         )
         total = finish(state)
         lowest = jnp.min(jnp.where(position >= 0, total, 1.0))
@@ -489,16 +530,14 @@
         @pl.when(lowest < LEAST)
         def _():
             def keep(chunk, best):
-                found = edge_score(chunk)
+                found = edge_score(chunk * per_chunk, per_chunk)
                 scores[chunk] = found
                 return jnp.maximum(best, jnp.max(found.reshape(CHUNK // 8, 8, wide), axis=0))
 
             best = lax.fori_loop(0, seen_chunks, keep, jnp.full((8, wide), MASKED, F32))
             best = jnp.max(best, axis=0, keepdims=True)
             finish(
-                lax.fori_loop(
-                    0, seen_chunks, lambda c, st: add(c, scores[c], best, st), nothing
-                )
+                lax.fori_loop(0, seen_chunks, lambda c, st: add(c * per_chunk, per_chunk, scores[c], best, st), nothing)
             )
 
         return carry
@@ -506,18 +545,19 @@
     lax.fori_loop(0, block_count[0], block_step, 0)
 
 
-def attend(tiles, block_count, positions, longest, received, keys, values_t, rows):
-    length = keys.shape[0]
+def attend(me, tiles, block_count, positions, received, mine, other, rows):
+    shards = received.shape[0]
     smem = pl.BlockSpec(memory_space=SMEM)
     vmem = pl.BlockSpec(memory_space=VMEM)
     block = 2 * TILES * 16
+    chunks = (mine.shape[0] - 1) * HEAD // CHUNK
     return pl.pallas_call(
         attend_kernel,
-        in_specs=[smem, smem, vmem, vmem, vmem, vmem, vmem],
+        in_specs=[smem, smem, smem, vmem, vmem, vmem, vmem],
         out_specs=vmem,
-        out_shape=jax.ShapeDtypeStruct((received.shape[0], 2 * rows, HEAD), BF16),
+        out_shape=jax.ShapeDtypeStruct((shards, 2 * rows, HEAD), BF16),
         scratch_shapes=[
-            pltpu.VMEM((length // CHUNK, CHUNK, block), F32),
+            pltpu.VMEM((chunks, CHUNK, block), F32),
             pltpu.VMEM((block, HEAD), BF16),
         ],
         compiler_params=params(28),
@@ -525,7 +565,7 @@
             flops=16000000000, bytes_accessed=3000000, transcendentals=0
         ),
         name="attend",
-    )(tiles, block_count, positions, longest, received, keys, values_t)
+    )(me, tiles, block_count, positions, received, mine, other)
 
 
 def place_cache_kernel(received, keys, values):
@@ -626,8 +666,7 @@
     mine, returned = blend(me, source, place, listed_lanes, received)
     other = lax.ppermute(mine, "shard", [(i, i ^ 1) for i in range(shards)])
     received_cache = exchange(returned)
-    keys, values_t, longest = turn(me, mine, other)
-    attended = attend(tiles, block_count, positions, longest, received, keys, values_t, rows)
+    attended = attend(me, tiles, block_count, positions, received, mine, other, rows)
     mixed_keys, mixed_values = place_cache(received_cache, own_pages, page_tokens)
     return mixed_keys, mixed_values, place_attended(exchange(attended))
 

time: 122 us -> 115 us (0.943)
  the two profiles are of different devices: /device:TPU:1 before, /device:TPU:193 now
where the time goes in v3:
time: 115 us; the launch traced here: 113 us
  Pallas kernels  53.8 us (47%)
  waiting for transfers between devices  36.9 us (32%)
  starting transfers between devices  19.8 us (17%)
  local copies, waits for them, and re-layouts  1.87 us (2%)
    all_to_all x3, waiting for transfers between devices, exchange(): return lax.all_to_all(blocks, 'shard', 0, 0)  36.9 us
    pallas_call x1, Pallas kernels, attend(): pl.pallas_call(attend_kernel, in_specs=[smem, smem, smem, vmem, vmem, vme...  33.1 us
    all_to_all x3, starting transfers between devices, exchange(): return lax.all_to_all(blocks, 'shard', 0, 0)  18.8 us
    pallas_call x1, Pallas kernels, plan(): pl.pallas_call(plan_kernel, in_specs=[smem, smem, smem, vmem], out_specs=...  8.43 us
    pallas_call x1, Pallas kernels, prepare(): pl.pallas_call(prepare_kernel, in_specs=[smem] * 5 + [vmem] + [anywhere]...  4.07 us
    pallas_call x1, Pallas kernels, blend(): pl.pallas_call(blend_kernel, in_specs=[smem, smem, smem, vmem, vmem], out...  4.05 us
    pallas_call x1, Pallas kernels, place_cache(): pl.pallas_call(place_cache_kernel, grid=(KV_HEADS,), in_specs=[pl.BlockSp...  2.62 us
  transfers between devices with their start and end apart: 4, of which 2 were waited for; matrix products, arithmetic and copies ran while one was open for 0% of the time, Pallas kernels for 39%

profile of v3, /device:TPU:193, one launch (start us, length us, event | category | flops | bytes accessed | tf_op | source)
XLA Modules:
  0.0 113.1 jit_solution(9797825577510269786)
XLA Ops:
  0.6 4.1 %prepare.1 = bf16[32,320,128]{2,1,0:T(8,128)(2,1)} custom-call(s32[1]{0:T(128)} %bitcast.me_ref, s32[352]{0:T(512)} %page_map.3, s32[8]{0:T(128)} %span_order.3, s32[1536]{0:T(1024)} %listed_index.1, f32[2,8,11]{2,1,0:T(8,128)} %bitcast.2, f32[1,128]{1,0:T(1,128)} %constant.8.clone.frequency, bf16[48,8192]{1,0:T(8,128)(2,1)} %queries_in.1, ...), custom_call_target="tpu_custom_call" | custom-call | flops 5000000000 | bytes 4300000 | tf_op jit(solution)/shard_map/prepare/pallas_call | solution.py:175
  4.7 0.0 copy-start.5
  4.7 0.0 copy-start.2
  4.7 0.0 copy-start.3
  4.8 0.0 copy-start.4
  4.8 7.9 %all-to-all-start = ((bf16[32,320,128]{2,1,0:T(8,128)(2,1)}), bf16[32,320,128]{2,1,0:T(8,128)(2,1)S(1)}, u32[]{:S(2)}, u32[]{:S(2)}) async-start(bf16[32,320,128]{2,1,0:T(8,128)(2,1)} %prepare.1), calls=%async_computation | async-start | bytes 5242880 | tf_op jit(solution)/shard_map/all_to_all | solution.py:624
  12.7 0.0 copy-done.5
  12.7 0.1 reshape.14
  12.8 0.0 copy-done.2
  12.8 0.1 fusion.listed_lanes
  12.8 0.0 copy-done.3
  12.8 0.0 copy-done.4
  12.8 8.4 %plan.1 = (s32[352]{0:T(512)S(1)}, s32[352]{0:T(512)S(1)}, s32[112]{0:T(128)S(1)}, s32[1]{0:T(128)}, s32[6,8,512]{2,1,0:T(8,128)S(1)}) custom-call(s32[352]{0:T(512)S(1)} %copy-done.3, s32[8]{0:T(128)S(1)} %copy-done.4, s32[32]{0:T(128)S(1)} %copy-done.2, s32[32,48]{1,0:T(8,128)S(1)} %fusion.listed_lanes), custom_call_target="tpu_custom_call" | custom-call | flops 8999999488 | bytes 3000000 | tf_op jit(solution)/shard_map/plan/pallas_call | solution.py:293
  21.3 25.3 %all-to-all-done.received = bf16[32,320,128]{2,1,0:T(8,128)(2,1)S(1)} async-done(((bf16[32,320,128]{2,1,0:T(8,128)(2,1)}), bf16[32,320,128]{2,1,0:T(8,128)(2,1)S(1)}, u32[]{:S(2)}, u32[]{:S(2)}) %all-to-all-start) | async-done | bytes 2621472 | tf_op jit(solution)/shard_map/all_to_all | solution.py:624
  46.6 4.0 %blend.1 = (bf16[45,128,128]{2,1,0:T(8,128)(2,1)}, bf16[32,96,128]{2,1,0:T(8,128)(2,1)S(1)}) custom-call(s32[1]{0:T(128)} %bitcast.me_ref, s32[352]{0:T(512)S(1)} %get-tuple-element.12.source, s32[352]{0:T(512)S(1)} %get-tuple-element.13.place, s32[32,48]{1,0:T(8,128)S(1)} %fusion.listed_lanes, bf16[32,320,128]{2,1,0:T(8,128)(2,1)S(1)} %all-to-all-done.received), custom_call_target="tpu_custom_call" | custom-call | flops 4000000000 | bytes 3000000 | tf_op jit(solution)/shard_map/blend/pallas_call | solution.py:389
  50.6 0.0 copy-start
  50.6 0.9 copy-done
  51.5 1.0 collective-permute-start
  52.5 3.7 %all-to-all-start.1 = ((bf16[32,96,128]{2,1,0:T(8,128)(2,1)}), bf16[32,96,128]{2,1,0:T(8,128)(2,1)S(1)}, u32[]{:S(2)}, u32[]{:S(2)}) async-start(bf16[32,96,128]{2,1,0:T(8,128)(2,1)} %copy-done), calls=%async_computation.1 | async-start | bytes 1572864 | tf_op jit(solution)/shard_map/all_to_all | solution.py:624
  56.2 0.0 collective-permute-done.other
  56.2 33.1 %attend.1 = bf16[32,96,128]{2,1,0:T(8,128)(2,1)S(1)} custom-call(s32[1]{0:T(128)} %bitcast.me_ref, s32[112]{0:T(128)S(1)} %get-tuple-element.17.tiles, s32[1]{0:T(128)} %get-tuple-element.18.block_count, s32[6,8,512]{2,1,0:T(8,128)S(1)} %get-tuple-element.19.positions, bf16[32,320,128]{2,1,0:T(8,128)(2,1)S(1)} %all-to-all-done.received, ...), custom_call_target="tpu_custom_call" | custom-call | flops 16000000000 | bytes 3000000 | tf_op jit(solution)/shard_map/attend/pallas_call | solution.py:554
  89.3 0.0 copy-start.1
  89.3 0.9 copy-done.1
  90.2 0.0 all-to-all-done.1.received
  90.2 7.2 %all-to-all-start.2 = ((bf16[32,96,128]{2,1,0:T(8,128)(2,1)}), bf16[32,96,128]{2,1,0:T(8,128)(2,1)S(1)}, u32[]{:S(2)}, u32[]{:S(2)}) async-start(bf16[32,96,128]{2,1,0:T(8,128)(2,1)} %copy-done.1), calls=%async_computation.2 | async-start | bytes 1572864 | tf_op jit(solution)/shard_map/all_to_all | solution.py:624
  97.4 2.6 %place_cache.1 = (bf16[11,16,1024]{2,1,0:T(8,128)(2,1)}, bf16[11,16,1024]{2,1,0:T(8,128)(2,1)}) custom-call(bf16[32,96,128]{2,1,0:T(8,128)(2,1)S(1)} %all-to-all-done.1.received), custom_call_target="tpu_custom_call" | custom-call | flops 2500000000 | bytes 3000000 | tf_op jit(solution)/shard_map/place_cache/pallas_call | solution.py:585
  100.0 11.6 %all-to-all-done.2.received = bf16[32,96,128]{2,1,0:T(8,128)(2,1)S(1)} async-done(((bf16[32,96,128]{2,1,0:T(8,128)(2,1)}), bf16[32,96,128]{2,1,0:T(8,128)(2,1)S(1)}, u32[]{:S(2)}, u32[]{:S(2)}) %all-to-all-start.2) | async-done | bytes 786464 | tf_op jit(solution)/shard_map/all_to_all | solution.py:624
  111.7 1.5 %place_attended.1 = bf16[48,8192]{1,0:T(8,128)(2,1)} custom-call(bf16[32,96,128]{2,1,0:T(8,128)(2,1)S(1)} %all-to-all-done.2.received), custom_call_target="tpu_custom_call" | custom-call | bytes 1600000 | tf_op jit(solution)/shard_map/place_attended/pallas_call | solution.py:611
Async XLA Ops:
  4.7 8.0 %copy-start.5 = (s32[1536]{0:T(1024)S(1)}, s32[1536]{0:T(1024)}, u32[]{:S(2)}) copy-start(s32[1536]{0:T(1024)} %listed_index.1) | copy-start | bytes 18436
  4.7 8.0 %copy-start.2 = (s32[32]{0:T(128)S(1)}, s32[32]{0:T(128)}, u32[]{:S(2)}) copy-start(s32[32]{0:T(128)} %listed_count.1) | copy-start | bytes 388
  4.7 8.1 %copy-start.3 = (s32[352]{0:T(512)S(1)}, s32[352]{0:T(512)}, u32[]{:S(2)}) copy-start(s32[352]{0:T(512)} %page_map.3) | copy-start | bytes 4228
  4.8 8.1 %copy-start.4 = (s32[8]{0:T(128)S(1)}, s32[8]{0:T(128)}, u32[]{:S(2)}) copy-start(s32[8]{0:T(128)} %span_order.3) | copy-start | bytes 100
  4.8 41.8 %all-to-all-start = ((bf16[32,320,128]{2,1,0:T(8,128)(2,1)}), bf16[32,320,128]{2,1,0:T(8,128)(2,1)S(1)}, u32[]{:S(2)}, u32[]{:S(2)}) async-start(bf16[32,320,128]{2,1,0:T(8,128)(2,1)} %prepare.1), calls=%async_computation | async-start | bytes 5242880 | tf_op jit(solution)/shard_map/all_to_all | solution.py:624
  50.6 0.9 copy-start
  51.5 4.7 %collective-permute-start = (bf16[45,128,128]{2,1,0:T(8,128)(2,1)}, bf16[45,128,128]{2,1,0:T(8,128)(2,1)}, u32[]{:S(2)}, u32[]{:S(2)}) collective-permute-start(bf16[45,128,128]{2,1,0:T(8,128)(2,1)} %get-tuple-element.20.mine), channel_id=1, source_target_pairs={{0,1},{1,0},{2,3},{3,2},{4,5},{5,4},{6,7},{7,6},{8,9},{9,8},{10,11... | collective-permute-start | bytes 4423688 | tf_op jit(solution)/shard_map/ppermute | solution.py:667
  52.5 37.8 %all-to-all-start.1 = ((bf16[32,96,128]{2,1,0:T(8,128)(2,1)}), bf16[32,96,128]{2,1,0:T(8,128)(2,1)S(1)}, u32[]{:S(2)}, u32[]{:S(2)}) async-start(bf16[32,96,128]{2,1,0:T(8,128)(2,1)} %copy-done), calls=%async_computation.1 | async-start | bytes 1572864 | tf_op jit(solution)/shard_map/all_to_all | solution.py:624
  89.3 0.9 copy-start.1
  90.2 21.4 %all-to-all-start.2 = ((bf16[32,96,128]{2,1,0:T(8,128)(2,1)}), bf16[32,96,128]{2,1,0:T(8,128)(2,1)S(1)}, u32[]{:S(2)}, u32[]{:S(2)}) async-start(bf16[32,96,128]{2,1,0:T(8,128)(2,1)} %copy-done.1), calls=%async_computation.2 | async-start | bytes 1572864 | tf_op jit(solution)/shard_map/all_to_all | solution.py:624

commit v4 on v3

--- a/solution.py
+++ b/solution.py
@@ -14,7 +14,8 @@
 ROPE_BASE = 1000000.0
 MASKED = -1e30
 VMEM_MIB = 56
-TILES = 16
+UNIT = 8
+UNITS = 32
 CHUNK = 1408
 PAGE = 16
 BIG = 22
@@ -239,22 +240,22 @@
         lax.fori_loop(0, per_span, note, 0, unroll=4)
 
     def count_tiles(shard, total):
-        return total + (listed_count[shard] + 15) // 16
+        return total + (listed_count[shard] + UNIT - 1) // UNIT
 
     total = lax.fori_loop(0, shards, count_tiles, 0)
-    blocks = (total + TILES - 1) // TILES
+    blocks = (total + UNITS - 1) // UNITS
     block_count[0] = blocks
-    for k in range(TILES):
+    for k in range(UNITS):
         tiles[k] = 0
 
     def list_tiles(shard, filled):
         count = listed_count[shard]
-        for k in range(rows // 16):
-            tiles[filled] = shard * (rows // 16) + k
-            filled = filled + jnp.where(count > 16 * k, 1, 0)
+        for k in range(rows // UNIT):
+            tiles[filled] = shard * 8 + k
+            filled = filled + jnp.where(count > UNIT * k, 1, 0)
         return filled
 
-    lax.fori_loop(0, shards, list_tiles, blocks * TILES - total)
+    lax.fori_loop(0, shards, list_tiles, blocks * UNITS - total)
 
     diagonal = lax.broadcasted_iota(I32, (rows, rows), 0) == lax.broadcasted_iota(
         I32, (rows, rows), 1
@@ -272,11 +273,12 @@
 
     def place_positions(b, carry):
         lanes = []
-        for t in range(0, TILES, 8):
+        for t in range(0, UNITS, HEAD // UNIT):
             found = []
-            for u in range(t, t + 8):
-                start = pl.multiple_of(tiles[b * TILES + u] * 16, 16)
-                found.append(row_position[pl.ds(start, 16), :])
+            for u in range(t, t + HEAD // UNIT):
+                code = tiles[b * UNITS + u]
+                start = pl.multiple_of((code >> 3) * rows + (code & 7) * UNIT, UNIT)
+                found.append(row_position[pl.ds(start, UNIT), :])
             lanes.append(jnp.concatenate(found, axis=0).T[:8])
         positions[b] = jnp.concatenate(lanes + lanes, axis=1).astype(I32)
         return carry
@@ -289,7 +291,7 @@
     smem = pl.BlockSpec(memory_space=SMEM)
     vmem = pl.BlockSpec(memory_space=VMEM)
     pages = page_map.shape[0]
-    block_limit = pl.cdiv(shards * (rows // 16), TILES)
+    block_limit = pl.cdiv(shards * (rows // UNIT), UNITS)
     return pl.pallas_call(
         plan_kernel,
         in_specs=[smem, smem, smem, vmem],
@@ -297,9 +299,9 @@
         out_shape=[
             jax.ShapeDtypeStruct((pages,), I32),
             jax.ShapeDtypeStruct((pages,), I32),
-            jax.ShapeDtypeStruct(((block_limit + 1) * TILES,), I32),
+            jax.ShapeDtypeStruct(((block_limit + 1) * UNITS,), I32),
             jax.ShapeDtypeStruct((1,), I32),
-            jax.ShapeDtypeStruct((block_limit, 8, 32 * TILES), I32),
+            jax.ShapeDtypeStruct((block_limit, 8, 2 * UNIT * UNITS), I32),
         ],
         scratch_shapes=[pltpu.VMEM((shards * rows, HEAD), F32)],
         compiler_params=params(16),
@@ -412,18 +414,24 @@
 
 
 def attend_kernel(
-    me_ref, tiles, block_count, positions, received, mine, other, out, scores, block
+    me_ref, tiles, block_count, positions, received, mine, other, out, scores, block, wide_out
 ):
     core = me_ref[0] % 2
-    out[...] = jnp.zeros_like(out)
+    wide_out[...] = jnp.zeros_like(wide_out)
 
     @pl.when(core == 0)
     def _():
-        attend_blocks(tiles, block_count, positions, received, mine, other, out, scores, block)
+        attend_blocks(
+            tiles, block_count, positions, received, mine, other, wide_out, scores, block
+        )
 
     @pl.when(core != 0)
     def _():
-        attend_blocks(tiles, block_count, positions, received, other, mine, out, scores, block)
+        attend_blocks(
+            tiles, block_count, positions, received, other, mine, wide_out, scores, block
+        )
+
+    out[...] = wide_out[...].astype(BF16)
 
 
 def attend_blocks(
@@ -433,25 +441,27 @@
     per_chunk = CHUNK // HEAD
     shards = out.shape[0]
     rows = out.shape[1] // 2
-    per_shard = rows // 16
     tokens = chunks * CHUNK // shards
-    half = TILES * 16
+    half = UNITS * UNIT
     wide = 2 * half
     top = keys[chunks * per_chunk, :1, :1].astype(F32)
     ones = jnp.ones((16, max(BIG, per_chunk) * HEAD), BF16)
 
     def block_step(b, carry):
-        first_tile = b * TILES
-        for t in range(TILES):
-            tile = tiles[first_tile + t]
-            shard = tile // per_shard
-            row = pl.multiple_of((tile - shard * per_shard) * 16, 16)
-            block[t * 16 : (t + 1) * 16] = received[shard, pl.ds(row, 16), :]
-            block[half + t * 16 : half + (t + 1) * 16] = received[shard, pl.ds(rows + row, 16), :]
-        open_keys = (tiles[first_tile] // per_shard) * tokens
-        seen_keys = (tiles[first_tile + TILES - 1] // per_shard + 1) * tokens
+        first_tile = b * UNITS
+        codes = [tiles[first_tile + t] for t in range(UNITS)]
+        for t in range(UNITS):
+            shard, unit = codes[t] >> 3, codes[t] & 7
+            odd = (unit & 1) == 1
+            for side in range(2):
+                row = pl.multiple_of(side * rows + (unit >> 1) * 16, 16)
+                pair = received[shard, pl.ds(row, 16), :].astype(F32)
+                at = side * half + t * UNIT
+                block[at : at + UNIT] = jnp.where(odd, pair[UNIT:], pair[:UNIT])
+        open_keys = (codes[0] >> 3) * tokens
+        seen_keys = ((codes[UNITS - 1] >> 3) + 1) * tokens
         seen_chunks = (seen_keys + CHUNK - 1) // CHUNK
-        query = block[...]
+        query = block[...].astype(BF16)
         position = positions[b][:1]
 
         def score(start, count):
@@ -477,15 +487,13 @@
         def finish(state):
             total = state[HEAD : HEAD + 1]
             result = state[:HEAD] / jnp.where(total > 0, total, 1.0)
-            result = jnp.where(position >= 0, result, 0.0).T.astype(BF16)
-            for t in range(TILES):
-                tile = tiles[first_tile + t]
-                shard = tile // per_shard
-                row = pl.multiple_of((tile - shard * per_shard) * 16, 16)
-                low = result[t * 16 : (t + 1) * 16]
-                high = result[half + t * 16 : half + (t + 1) * 16]
-                out[shard, pl.ds(row, 16), :] = low
-                out[shard, pl.ds(rows + row, 16), :] = high
+            result = jnp.where(position >= 0, result, 0.0).T
+            for t in range(UNITS):
+                shard, unit = codes[t] >> 3, codes[t] & 7
+                for side in range(2):
+                    row = pl.multiple_of(side * rows + unit * UNIT, UNIT)
+                    at = side * half + t * UNIT
+                    out[shard, pl.ds(row, UNIT), :] = result[at : at + UNIT]
             return total
 
         nothing = jnp.zeros((HEAD + 16, wide), F32)
@@ -549,7 +557,7 @@
     shards = received.shape[0]
     smem = pl.BlockSpec(memory_space=SMEM)
     vmem = pl.BlockSpec(memory_space=VMEM)
-    block = 2 * TILES * 16
+    block = 2 * UNITS * UNIT
     chunks = (mine.shape[0] - 1) * HEAD // CHUNK
     return pl.pallas_call(
         attend_kernel,
@@ -558,7 +566,8 @@
         out_shape=jax.ShapeDtypeStruct((shards, 2 * rows, HEAD), BF16),
         scratch_shapes=[
             pltpu.VMEM((chunks, CHUNK, block), F32),
-            pltpu.VMEM((block, HEAD), BF16),
+            pltpu.VMEM((block, HEAD), F32),
+            pltpu.VMEM((shards, 2 * rows, HEAD), F32),
         ],
         compiler_params=params(28),
         cost_estimate=pl.CostEstimate(

time: 115 us -> 111 us (0.965)
  the two profiles are of different devices: /device:TPU:193 before, /device:TPU:161 now
where the time goes in v4:
time: 111 us; the launch traced here: 110 us
  Pallas kernels  51.3 us (46%)
  waiting for transfers between devices  36.7 us (33%)
  starting transfers between devices  19.7 us (18%)
  local copies, waits for them, and re-layouts  1.87 us (2%)
    all_to_all x3, waiting for transfers between devices, exchange(): return lax.all_to_all(blocks, 'shard', 0, 0)  36.7 us
    pallas_call x1, Pallas kernels, attend(): pl.pallas_call(attend_kernel, in_specs=[smem, smem, smem, vmem, vmem, vme...  30.5 us
    all_to_all x3, starting transfers between devices, exchange(): return lax.all_to_all(blocks, 'shard', 0, 0)  18.8 us
    pallas_call x1, Pallas kernels, plan(): pl.pallas_call(plan_kernel, in_specs=[smem, smem, smem, vmem], out_specs=...  8.61 us
    pallas_call x1, Pallas kernels, prepare(): pl.pallas_call(prepare_kernel, in_specs=[smem] * 5 + [vmem] + [anywhere]...  4.07 us
    pallas_call x1, Pallas kernels, blend(): pl.pallas_call(blend_kernel, in_specs=[smem, smem, smem, vmem, vmem], out...  4.05 us
    pallas_call x1, Pallas kernels, place_cache(): pl.pallas_call(place_cache_kernel, grid=(KV_HEADS,), in_specs=[pl.BlockSp...  2.62 us
  transfers between devices with their start and end apart: 4, of which 2 were waited for; matrix products, arithmetic and copies ran while one was open for 0% of the time, Pallas kernels for 38%

profile of v4, /device:TPU:161, one launch (start us, length us, event | category | flops | bytes accessed | tf_op | source)
XLA Modules:
  0.0 110.5 jit_solution(14204785332578285470)
XLA Ops:
  0.6 4.1 %prepare.1 = bf16[32,320,128]{2,1,0:T(8,128)(2,1)} custom-call(s32[1]{0:T(128)} %bitcast.me_ref, s32[352]{0:T(512)} %page_map.3, s32[8]{0:T(128)} %span_order.3, s32[1536]{0:T(1024)} %listed_index.1, f32[2,8,11]{2,1,0:T(8,128)} %bitcast.2, f32[1,128]{1,0:T(1,128)} %constant.8.clone.frequency, bf16[48,8192]{1,0:T(8,128)(2,1)} %queries_in.1, ...), custom_call_target="tpu_custom_call" | custom-call | flops 5000000000 | bytes 4300000 | tf_op jit(solution)/shard_map/prepare/pallas_call | solution.py:176
  4.7 0.0 copy-start.5
  4.7 0.0 copy-start.2
  4.7 0.0 copy-start.3
  4.8 0.0 copy-start.4
  4.8 7.9 %all-to-all-start = ((bf16[32,320,128]{2,1,0:T(8,128)(2,1)}), bf16[32,320,128]{2,1,0:T(8,128)(2,1)S(1)}, u32[]{:S(2)}, u32[]{:S(2)}) async-start(bf16[32,320,128]{2,1,0:T(8,128)(2,1)} %prepare.1), calls=%async_computation | async-start | bytes 5242880 | tf_op jit(solution)/shard_map/all_to_all | solution.py:633
  12.7 0.0 copy-done.5
  12.7 0.1 reshape.14
  12.8 0.0 copy-done.2
  12.8 0.1 fusion.listed_lanes
  12.8 0.0 copy-done.3
  12.8 0.0 copy-done.4
  12.8 8.6 %plan.1 = (s32[352]{0:T(512)S(1)}, s32[352]{0:T(512)S(1)}, s32[224]{0:T(256)S(1)}, s32[1]{0:T(128)}, s32[6,8,512]{2,1,0:T(8,128)S(1)}) custom-call(s32[352]{0:T(512)S(1)} %copy-done.3, s32[8]{0:T(128)S(1)} %copy-done.4, s32[32]{0:T(128)S(1)} %copy-done.2, s32[32,48]{1,0:T(8,128)S(1)} %fusion.listed_lanes), custom_call_target="tpu_custom_call" | custom-call | flops 8999999488 | bytes 3000000 | tf_op jit(solution)/shard_map/plan/pallas_call | solution.py:295
  21.5 25.1 %all-to-all-done.received = bf16[32,320,128]{2,1,0:T(8,128)(2,1)S(1)} async-done(((bf16[32,320,128]{2,1,0:T(8,128)(2,1)}), bf16[32,320,128]{2,1,0:T(8,128)(2,1)S(1)}, u32[]{:S(2)}, u32[]{:S(2)}) %all-to-all-start) | async-done | bytes 2621472 | tf_op jit(solution)/shard_map/all_to_all | solution.py:633
  46.6 4.1 %blend.1 = (bf16[45,128,128]{2,1,0:T(8,128)(2,1)}, bf16[32,96,128]{2,1,0:T(8,128)(2,1)S(1)}) custom-call(s32[1]{0:T(128)} %bitcast.me_ref, s32[352]{0:T(512)S(1)} %get-tuple-element.12.source, s32[352]{0:T(512)S(1)} %get-tuple-element.13.place, s32[32,48]{1,0:T(8,128)S(1)} %fusion.listed_lanes, bf16[32,320,128]{2,1,0:T(8,128)(2,1)S(1)} %all-to-all-done.received), custom_call_target="tpu_custom_call" | custom-call | flops 4000000000 | bytes 3000000 | tf_op jit(solution)/shard_map/blend/pallas_call | solution.py:391
  50.6 0.0 copy-start
  50.6 0.9 copy-done
  51.5 1.0 collective-permute-start
  52.5 3.7 %all-to-all-start.1 = ((bf16[32,96,128]{2,1,0:T(8,128)(2,1)}), bf16[32,96,128]{2,1,0:T(8,128)(2,1)S(1)}, u32[]{:S(2)}, u32[]{:S(2)}) async-start(bf16[32,96,128]{2,1,0:T(8,128)(2,1)} %copy-done), calls=%async_computation.1 | async-start | bytes 1572864 | tf_op jit(solution)/shard_map/all_to_all | solution.py:633
  56.2 0.0 collective-permute-done.other
  56.2 30.5 %attend.1 = bf16[32,96,128]{2,1,0:T(8,128)(2,1)S(1)} custom-call(s32[1]{0:T(128)} %bitcast.me_ref, s32[224]{0:T(256)S(1)} %get-tuple-element.17.tiles, s32[1]{0:T(128)} %get-tuple-element.18.block_count, s32[6,8,512]{2,1,0:T(8,128)S(1)} %get-tuple-element.19.positions, bf16[32,320,128]{2,1,0:T(8,128)(2,1)S(1)} %all-to-all-done.received, ...), custom_call_target="tpu_custom_call" | custom-call | flops 16000000000 | bytes 3000000 | tf_op jit(solution)/shard_map/attend/pallas_call | solution.py:562
  86.7 0.0 copy-start.1
  86.7 0.9 copy-done.1
  87.6 0.0 all-to-all-done.1.received
  87.6 7.2 %all-to-all-start.2 = ((bf16[32,96,128]{2,1,0:T(8,128)(2,1)}), bf16[32,96,128]{2,1,0:T(8,128)(2,1)S(1)}, u32[]{:S(2)}, u32[]{:S(2)}) async-start(bf16[32,96,128]{2,1,0:T(8,128)(2,1)} %copy-done.1), calls=%async_computation.2 | async-start | bytes 1572864 | tf_op jit(solution)/shard_map/all_to_all | solution.py:633
  94.8 2.6 %place_cache.1 = (bf16[11,16,1024]{2,1,0:T(8,128)(2,1)}, bf16[11,16,1024]{2,1,0:T(8,128)(2,1)}) custom-call(bf16[32,96,128]{2,1,0:T(8,128)(2,1)S(1)} %all-to-all-done.1.received), custom_call_target="tpu_custom_call" | custom-call | flops 2500000000 | bytes 3000000 | tf_op jit(solution)/shard_map/place_cache/pallas_call | solution.py:594
  97.4 11.6 %all-to-all-done.2.received = bf16[32,96,128]{2,1,0:T(8,128)(2,1)S(1)} async-done(((bf16[32,96,128]{2,1,0:T(8,128)(2,1)}), bf16[32,96,128]{2,1,0:T(8,128)(2,1)S(1)}, u32[]{:S(2)}, u32[]{:S(2)}) %all-to-all-start.2) | async-done | bytes 786464 | tf_op jit(solution)/shard_map/all_to_all | solution.py:633
  109.0 1.5 %place_attended.1 = bf16[48,8192]{1,0:T(8,128)(2,1)} custom-call(bf16[32,96,128]{2,1,0:T(8,128)(2,1)S(1)} %all-to-all-done.2.received), custom_call_target="tpu_custom_call" | custom-call | bytes 1600000 | tf_op jit(solution)/shard_map/place_attended/pallas_call | solution.py:620
Async XLA Ops:
  4.7 8.0 %copy-start.5 = (s32[1536]{0:T(1024)S(1)}, s32[1536]{0:T(1024)}, u32[]{:S(2)}) copy-start(s32[1536]{0:T(1024)} %listed_index.1) | copy-start | bytes 18436
  4.7 8.0 %copy-start.2 = (s32[32]{0:T(128)S(1)}, s32[32]{0:T(128)}, u32[]{:S(2)}) copy-start(s32[32]{0:T(128)} %listed_count.1) | copy-start | bytes 388
  4.7 8.1 %copy-start.3 = (s32[352]{0:T(512)S(1)}, s32[352]{0:T(512)}, u32[]{:S(2)}) copy-start(s32[352]{0:T(512)} %page_map.3) | copy-start | bytes 4228
  4.8 8.1 %copy-start.4 = (s32[8]{0:T(128)S(1)}, s32[8]{0:T(128)}, u32[]{:S(2)}) copy-start(s32[8]{0:T(128)} %span_order.3) | copy-start | bytes 100
  4.8 41.8 %all-to-all-start = ((bf16[32,320,128]{2,1,0:T(8,128)(2,1)}), bf16[32,320,128]{2,1,0:T(8,128)(2,1)S(1)}, u32[]{:S(2)}, u32[]{:S(2)}) async-start(bf16[32,320,128]{2,1,0:T(8,128)(2,1)} %prepare.1), calls=%async_computation | async-start | bytes 5242880 | tf_op jit(solution)/shard_map/all_to_all | solution.py:633
  50.6 0.9 copy-start
  51.5 4.7 %collective-permute-start = (bf16[45,128,128]{2,1,0:T(8,128)(2,1)}, bf16[45,128,128]{2,1,0:T(8,128)(2,1)}, u32[]{:S(2)}, u32[]{:S(2)}) collective-permute-start(bf16[45,128,128]{2,1,0:T(8,128)(2,1)} %get-tuple-element.20.mine), channel_id=1, source_target_pairs={{0,1},{1,0},{2,3},{3,2},{4,5},{5,4},{6,7},{7,6},{8,9},{9,8},{10,11... | collective-permute-start | bytes 4423688 | tf_op jit(solution)/shard_map/ppermute | solution.py:676
  52.5 35.1 %all-to-all-start.1 = ((bf16[32,96,128]{2,1,0:T(8,128)(2,1)}), bf16[32,96,128]{2,1,0:T(8,128)(2,1)S(1)}, u32[]{:S(2)}, u32[]{:S(2)}) async-start(bf16[32,96,128]{2,1,0:T(8,128)(2,1)} %copy-done), calls=%async_computation.1 | async-start | bytes 1572864 | tf_op jit(solution)/shard_map/all_to_all | solution.py:633
  86.7 0.9 copy-start.1
  87.6 21.4 %all-to-all-start.2 = ((bf16[32,96,128]{2,1,0:T(8,128)(2,1)}), bf16[32,96,128]{2,1,0:T(8,128)(2,1)S(1)}, u32[]{:S(2)}, u32[]{:S(2)}) async-start(bf16[32,96,128]{2,1,0:T(8,128)(2,1)} %copy-done.1), calls=%async_computation.2 | async-start | bytes 1572864 | tf_op jit(solution)/shard_map/all_to_all | solution.py:633

commit v5 on v4

--- a/solution.py
+++ b/solution.py
@@ -18,9 +18,6 @@
 UNITS = 32
 CHUNK = 1408
 PAGE = 16
-BIG = 22
-MID = 11
-SMALL = 4
 EXP2_SCALE = float(HEAD**-0.5 / np.log(2.0))
 
 BF16 = jnp.bfloat16
@@ -89,7 +86,6 @@
         pltpu.make_async_copy(source, target, in_sems.at[i])
         for i, (source, target) in enumerate(
             (
-                (queries_in, queries),
                 (keys_in, keys),
                 (values_in, values),
                 (fresh_keys_in, fresh_keys),
@@ -97,7 +93,16 @@
             )
         )
     ]
-    for arrival in arrivals:
+    query_arrivals = []
+    for head in range(KV_HEADS):
+        wide = queries.shape[1] // KV_HEADS
+        lanes = pl.ds(head * wide, wide)
+        query_arrivals.append(
+            pltpu.make_async_copy(
+                queries_in.at[:, lanes], queries.at[:, lanes], in_sems.at[len(arrivals) + head]
+            )
+        )
+    for arrival in arrivals + query_arrivals:
         arrival.start()
 
     for c in range(rows):
@@ -125,6 +130,7 @@
     for head in range(KV_HEADS):
         lanes = slice(head * HEAD, (head + 1) * HEAD)
         outs = [head * group + j for j in range(group)]
+        query_arrivals[head].wait()
         for j in range(group):
             for t in range(2):
                 at = (2 * (head * group + j) + t) * HEAD
@@ -185,7 +191,7 @@
             pltpu.VMEM((rows, HEAD), F32),
             pltpu.VMEM((span_order.shape[0], HEAD), F32),
             pltpu.VMEM((span_order.shape[0], HEAD), F32),
-            pltpu.SemaphoreType.DMA((len(arrays),)),
+            pltpu.SemaphoreType.DMA((len(arrays) - 1 + KV_HEADS,)),
             pltpu.SemaphoreType.DMA((KV_HEADS,)),
         ],
         compiler_params=params(VMEM_MIB),
@@ -414,7 +420,7 @@
 
 
 def attend_kernel(
-    me_ref, tiles, block_count, positions, received, mine, other, out, scores, block, wide_out
+    me_ref, tiles, block_count, positions, received, mine, other, out, block, wide_out
 ):
     core = me_ref[0] % 2
     wide_out[...] = jnp.zeros_like(wide_out)
@@ -422,30 +428,30 @@
     @pl.when(core == 0)
     def _():
         attend_blocks(
-            tiles, block_count, positions, received, mine, other, wide_out, scores, block
+            tiles, block_count, positions, received, mine, other, wide_out, block
         )
 
     @pl.when(core != 0)
     def _():
         attend_blocks(
-            tiles, block_count, positions, received, other, mine, wide_out, scores, block
+            tiles, block_count, positions, received, other, mine, wide_out, block
         )
 
     out[...] = wide_out[...].astype(BF16)
 
 
 def attend_blocks(
-    tiles, block_count, positions, received, keys, values_t, out, scores, block
+    tiles, block_count, positions, received, keys, values_t, out, block
 ):
-    chunks = scores.shape[0]
     per_chunk = CHUNK // HEAD
+    chunks = keys.shape[0] // per_chunk
     shards = out.shape[0]
     rows = out.shape[1] // 2
     tokens = chunks * CHUNK // shards
     half = UNITS * UNIT
     wide = 2 * half
     top = keys[chunks * per_chunk, :1, :1].astype(F32)
-    ones = jnp.ones((16, max(BIG, per_chunk) * HEAD), BF16)
+    ones = jnp.ones((16, chunks * CHUNK), BF16)
 
     def block_step(b, carry):
         first_tile = b * UNITS
@@ -458,7 +464,6 @@
                 pair = received[shard, pl.ds(row, 16), :].astype(F32)
                 at = side * half + t * UNIT
                 block[at : at + UNIT] = jnp.where(odd, pair[UNIT:], pair[:UNIT])
-        open_keys = (codes[0] >> 3) * tokens
         seen_keys = ((codes[UNITS - 1] >> 3) + 1) * tokens
         seen_chunks = (seen_keys + CHUNK - 1) // CHUNK
         query = block[...].astype(BF16)
@@ -505,32 +510,12 @@
             preferred_element_type=F32,
         )
         bound = jnp.sqrt(squares[:1] * top) * (1.02 * EXP2_SCALE) - SLACK
-        seen = seen_keys // PAGE
-        big, mid, small = BIG * HEAD // PAGE, MID * HEAD // PAGE, SMALL * HEAD // PAGE
-        big_steps = seen // big
-        rest = seen - big_steps * big
-        big_steps = big_steps + jnp.where(rest > mid + small, 1, 0)
-        rest = jnp.where(rest > mid + small, 0, rest)
-        mid_steps = jnp.where(rest > small, 1, 0)
-        small_steps = jnp.where(rest > mid_steps * mid, 1, 0)
-        open_steps = open_keys // (BIG * HEAD)
-        mid_from = big_steps * BIG
-        small_from = mid_from + mid_steps * MID
-
-        def open_step(c, st):
-            start = c * BIG
-            return add(start, BIG, score(start, BIG), bound, st)
-
-        def edge_step(start, count, st):
-            return add(start, count, edge_score(start, count), bound, st)
-
-        state = lax.fori_loop(0, open_steps, open_step, nothing)
-        state = lax.fori_loop(
-            open_steps, big_steps, lambda c, st: edge_step(c * BIG, BIG, st), state
-        )
-        state = lax.fori_loop(0, mid_steps, lambda c, st: edge_step(mid_from, MID, st), state)
-        state = lax.fori_loop(
-            0, small_steps, lambda c, st: edge_step(small_from, SMALL, st), state
+        def whole(count):
+            return lambda: add(0, count, edge_score(0, count), bound, nothing)
+
+        state = lax.switch(
+            jnp.maximum(seen_chunks, 1) - 1,
+            [whole((c + 1) * per_chunk) for c in range(chunks)],
         )
         total = finish(state)
         lowest = jnp.min(jnp.where(position >= 0, total, 1.0))
@@ -539,14 +524,16 @@
         def _():
             def keep(chunk, best):
                 found = edge_score(chunk * per_chunk, per_chunk)
-                scores[chunk] = found
                 return jnp.maximum(best, jnp.max(found.reshape(CHUNK // 8, 8, wide), axis=0))
 
             best = lax.fori_loop(0, seen_chunks, keep, jnp.full((8, wide), MASKED, F32))
             best = jnp.max(best, axis=0, keepdims=True)
-            finish(
-                lax.fori_loop(0, seen_chunks, lambda c, st: add(c * per_chunk, per_chunk, scores[c], best, st), nothing)
-            )
+
+            def again(chunk, st):
+                start = chunk * per_chunk
+                return add(start, per_chunk, edge_score(start, per_chunk), best, st)
+
+            finish(lax.fori_loop(0, seen_chunks, again, nothing))
 
         return carry
 
@@ -558,18 +545,16 @@
     smem = pl.BlockSpec(memory_space=SMEM)
     vmem = pl.BlockSpec(memory_space=VMEM)
     block = 2 * UNITS * UNIT
-    chunks = (mine.shape[0] - 1) * HEAD // CHUNK
     return pl.pallas_call(
         attend_kernel,
         in_specs=[smem, smem, smem, vmem, vmem, vmem, vmem],
         out_specs=vmem,
         out_shape=jax.ShapeDtypeStruct((shards, 2 * rows, HEAD), BF16),
         scratch_shapes=[
-            pltpu.VMEM((chunks, CHUNK, block), F32),
             pltpu.VMEM((block, HEAD), F32),
             pltpu.VMEM((shards, 2 * rows, HEAD), F32),
         ],
-        compiler_params=params(28),
+        compiler_params=params(32),
         cost_estimate=pl.CostEstimate(
             flops=16000000000, bytes_accessed=3000000, transcendentals=0
         ),
@@ -605,24 +590,25 @@
     )(received)
 
 
-def place_attended_kernel(received, out):
+def place_attended_kernel(received, out, sem):
     rows = out.shape[0]
-    for j in range(received.shape[0]):
-        for t in range(2):
-            head = 2 * j + t
-            out[:, head * HEAD : (head + 1) * HEAD] = received[j, t * rows : (t + 1) * rows]
+    for head in range(2 * received.shape[0]):
+        row, lane = head % 2 * rows, head * HEAD
+        pltpu.make_async_copy(
+            received.at[head // 2, pl.ds(row, rows)], out.at[:, pl.ds(lane, HEAD)], sem
+        ).start()
+    pltpu.make_async_copy(out, out, sem).wait()
 
 
 def place_attended(received):
     shards, sent, _ = received.shape
-    steps = 4
-    rows, width = sent // 2, shards * 2 * HEAD
+    anywhere = pl.BlockSpec(memory_space=pl.ANY)
     return pl.pallas_call(
         place_attended_kernel,
-        grid=(steps,),
-        in_specs=[pl.BlockSpec((shards // steps, sent, HEAD), lambda h: (h, 0, 0))],
-        out_specs=pl.BlockSpec((rows, width // steps), lambda h: (0, h)),
-        out_shape=jax.ShapeDtypeStruct((rows, width), BF16),
+        in_specs=[anywhere],
+        out_specs=anywhere,
+        out_shape=jax.ShapeDtypeStruct((sent // 2, shards * 2 * HEAD), BF16),
+        scratch_shapes=[pltpu.SemaphoreType.DMA],
         compiler_params=params(16),
         cost_estimate=pl.CostEstimate(flops=0, bytes_accessed=1600000, transcendentals=0),
         name="place_attended",

time: 111 us -> 112 us (level)
  the two profiles are of different devices: /device:TPU:161 before, /device:TPU:1 now
where the time goes in v5:
time: 112 us
  Pallas kernels  51.4 us (46%)
  waiting for transfers between devices  36.7 us (33%)
  starting transfers between devices  21.1 us (19%)
  local copies, waits for them, and re-layouts  1.87 us (2%)
    all_to_all x3, waiting for transfers between devices, exchange(): return lax.all_to_all(blocks, 'shard', 0, 0)  36.7 us
    pallas_call x1, Pallas kernels, attend(): pl.pallas_call(attend_kernel, in_specs=[smem, smem, smem, vmem, vmem, vme...  31.2 us
    all_to_all x3, starting transfers between devices, exchange(): return lax.all_to_all(blocks, 'shard', 0, 0)  20.1 us
    pallas_call x1, Pallas kernels, plan(): pl.pallas_call(plan_kernel, in_specs=[smem, smem, smem, vmem], out_specs=...  8.61 us
    pallas_call x1, Pallas kernels, prepare(): pl.pallas_call(prepare_kernel, in_specs=[smem] * 5 + [vmem] + [anywhere]...  4.07 us
    pallas_call x1, Pallas kernels, blend(): pl.pallas_call(blend_kernel, in_specs=[smem, smem, smem, vmem, vmem], out...  4.05 us
    pallas_call x1, Pallas kernels, place_cache(): pl.pallas_call(place_cache_kernel, grid=(KV_HEADS,), in_specs=[pl.BlockSp...  2.62 us
  transfers between devices with their start and end apart: 4, of which 2 were waited for; matrix products, arithmetic and copies ran while one was open for 0% of the time, Pallas kernels for 38%

profile of v5, /device:TPU:1, one launch (start us, length us, event | category | flops | bytes accessed | tf_op | source)
XLA Modules:
  0.0 112.1 jit_solution(10120997887075958750)
XLA Ops:
  0.6 4.1 %prepare.1 = bf16[32,320,128]{2,1,0:T(8,128)(2,1)} custom-call(s32[1]{0:T(128)} %bitcast.me_ref, s32[352]{0:T(512)} %page_map.3, s32[8]{0:T(128)} %span_order.3, s32[1536]{0:T(1024)} %listed_index.1, f32[2,8,11]{2,1,0:T(8,128)} %bitcast.2, f32[1,128]{1,0:T(1,128)} %constant.8.clone.frequency, bf16[48,8192]{1,0:T(8,128)(2,1)} %queries_in.1, ...), custom_call_target="tpu_custom_call" | custom-call | flops 5000000000 | bytes 4300000 | tf_op jit(solution)/shard_map/prepare/pallas_call | solution.py:182
  4.7 0.0 copy-start.5
  4.7 0.0 copy-start.2
  4.7 0.0 copy-start.3
  4.7 0.0 copy-start.4
  4.8 8.7 %all-to-all-start = ((bf16[32,320,128]{2,1,0:T(8,128)(2,1)}), bf16[32,320,128]{2,1,0:T(8,128)(2,1)S(1)}, u32[]{:S(2)}, u32[]{:S(2)}) async-start(bf16[32,320,128]{2,1,0:T(8,128)(2,1)} %prepare.1), calls=%async_computation | async-start | bytes 5242880 | tf_op jit(solution)/shard_map/all_to_all | solution.py:619
  13.5 0.0 copy-done.5
  13.5 0.1 reshape.14
  13.6 0.0 copy-done.2
  13.6 0.1 fusion.listed_lanes
  13.7 0.0 copy-done.3
  13.7 0.0 copy-done.4
  13.7 8.6 %plan.1 = (s32[352]{0:T(512)S(1)}, s32[352]{0:T(512)S(1)}, s32[224]{0:T(256)S(1)}, s32[1]{0:T(128)}, s32[6,8,512]{2,1,0:T(8,128)S(1)}) custom-call(s32[352]{0:T(512)S(1)} %copy-done.3, s32[8]{0:T(128)S(1)} %copy-done.4, s32[32]{0:T(128)S(1)} %copy-done.2, s32[32,48]{1,0:T(8,128)S(1)} %fusion.listed_lanes), custom_call_target="tpu_custom_call" | custom-call | flops 8999999488 | bytes 3000000 | tf_op jit(solution)/shard_map/plan/pallas_call | solution.py:301
  22.3 25.1 %all-to-all-done.received = bf16[32,320,128]{2,1,0:T(8,128)(2,1)S(1)} async-done(((bf16[32,320,128]{2,1,0:T(8,128)(2,1)}), bf16[32,320,128]{2,1,0:T(8,128)(2,1)S(1)}, u32[]{:S(2)}, u32[]{:S(2)}) %all-to-all-start) | async-done | bytes 2621472 | tf_op jit(solution)/shard_map/all_to_all | solution.py:619
  47.4 4.0 %blend.1 = (bf16[45,128,128]{2,1,0:T(8,128)(2,1)}, bf16[32,96,128]{2,1,0:T(8,128)(2,1)S(1)}) custom-call(s32[1]{0:T(128)} %bitcast.me_ref, s32[352]{0:T(512)S(1)} %get-tuple-element.12.source, s32[352]{0:T(512)S(1)} %get-tuple-element.13.place, s32[32,48]{1,0:T(8,128)S(1)} %fusion.listed_lanes, bf16[32,320,128]{2,1,0:T(8,128)(2,1)S(1)} %all-to-all-done.received), custom_call_target="tpu_custom_call" | custom-call | flops 4000000000 | bytes 3000000 | tf_op jit(solution)/shard_map/blend/pallas_call | solution.py:397
  51.4 0.0 copy-start
  51.5 0.9 copy-done
  52.3 1.0 collective-permute-start
  53.3 3.7 %all-to-all-start.1 = ((bf16[32,96,128]{2,1,0:T(8,128)(2,1)}), bf16[32,96,128]{2,1,0:T(8,128)(2,1)S(1)}, u32[]{:S(2)}, u32[]{:S(2)}) async-start(bf16[32,96,128]{2,1,0:T(8,128)(2,1)} %copy-done), calls=%async_computation.1 | async-start | bytes 1572864 | tf_op jit(solution)/shard_map/all_to_all | solution.py:619
  57.0 0.0 collective-permute-done.other
  57.0 31.2 %attend.1 = bf16[32,96,128]{2,1,0:T(8,128)(2,1)S(1)} custom-call(s32[1]{0:T(128)} %bitcast.me_ref, s32[224]{0:T(256)S(1)} %get-tuple-element.17.tiles, s32[1]{0:T(128)} %get-tuple-element.18.block_count, s32[6,8,512]{2,1,0:T(8,128)S(1)} %get-tuple-element.19.positions, bf16[32,320,128]{2,1,0:T(8,128)(2,1)S(1)} %all-to-all-done.received, ...), custom_call_target="tpu_custom_call" | custom-call | flops 16000000000 | bytes 3000000 | tf_op jit(solution)/shard_map/attend/pallas_call | solution.py:548
  88.2 0.0 copy-start.1
  88.2 0.9 copy-done.1
  89.1 0.0 all-to-all-done.1.received
  89.1 7.7 %all-to-all-start.2 = ((bf16[32,96,128]{2,1,0:T(8,128)(2,1)}), bf16[32,96,128]{2,1,0:T(8,128)(2,1)S(1)}, u32[]{:S(2)}, u32[]{:S(2)}) async-start(bf16[32,96,128]{2,1,0:T(8,128)(2,1)} %copy-done.1), calls=%async_computation.2 | async-start | bytes 1572864 | tf_op jit(solution)/shard_map/all_to_all | solution.py:619
  96.8 2.6 %place_cache.1 = (bf16[11,16,1024]{2,1,0:T(8,128)(2,1)}, bf16[11,16,1024]{2,1,0:T(8,128)(2,1)}) custom-call(bf16[32,96,128]{2,1,0:T(8,128)(2,1)S(1)} %all-to-all-done.1.received), custom_call_target="tpu_custom_call" | custom-call | flops 2500000000 | bytes 3000000 | tf_op jit(solution)/shard_map/place_cache/pallas_call | solution.py:579
  99.4 11.6 %all-to-all-done.2.received = bf16[32,96,128]{2,1,0:T(8,128)(2,1)S(1)} async-done(((bf16[32,96,128]{2,1,0:T(8,128)(2,1)}), bf16[32,96,128]{2,1,0:T(8,128)(2,1)S(1)}, u32[]{:S(2)}, u32[]{:S(2)}) %all-to-all-start.2) | async-done | bytes 786464 | tf_op jit(solution)/shard_map/all_to_all | solution.py:619
  111.0 0.8 place_attended.1
Async XLA Ops:
  4.7 8.8 %copy-start.5 = (s32[1536]{0:T(1024)S(1)}, s32[1536]{0:T(1024)}, u32[]{:S(2)}) copy-start(s32[1536]{0:T(1024)} %listed_index.1) | copy-start | bytes 18436
  4.7 8.9 %copy-start.2 = (s32[32]{0:T(128)S(1)}, s32[32]{0:T(128)}, u32[]{:S(2)}) copy-start(s32[32]{0:T(128)} %listed_count.1) | copy-start | bytes 388
  4.7 8.9 %copy-start.3 = (s32[352]{0:T(512)S(1)}, s32[352]{0:T(512)}, u32[]{:S(2)}) copy-start(s32[352]{0:T(512)} %page_map.3) | copy-start | bytes 4228
  4.7 8.9 %copy-start.4 = (s32[8]{0:T(128)S(1)}, s32[8]{0:T(128)}, u32[]{:S(2)}) copy-start(s32[8]{0:T(128)} %span_order.3) | copy-start | bytes 100
  4.8 42.6 %all-to-all-start = ((bf16[32,320,128]{2,1,0:T(8,128)(2,1)}), bf16[32,320,128]{2,1,0:T(8,128)(2,1)S(1)}, u32[]{:S(2)}, u32[]{:S(2)}) async-start(bf16[32,320,128]{2,1,0:T(8,128)(2,1)} %prepare.1), calls=%async_computation | async-start | bytes 5242880 | tf_op jit(solution)/shard_map/all_to_all | solution.py:619
  51.4 0.9 copy-start
  52.3 4.7 %collective-permute-start = (bf16[45,128,128]{2,1,0:T(8,128)(2,1)}, bf16[45,128,128]{2,1,0:T(8,128)(2,1)}, u32[]{:S(2)}, u32[]{:S(2)}) collective-permute-start(bf16[45,128,128]{2,1,0:T(8,128)(2,1)} %get-tuple-element.20.mine), channel_id=1, source_target_pairs={{0,1},{1,0},{2,3},{3,2},{4,5},{5,4},{6,7},{7,6},{8,9},{9,8},{10,11... | collective-permute-start | bytes 4423688 | tf_op jit(solution)/shard_map/ppermute | solution.py:662
  53.3 35.8 %all-to-all-start.1 = ((bf16[32,96,128]{2,1,0:T(8,128)(2,1)}), bf16[32,96,128]{2,1,0:T(8,128)(2,1)S(1)}, u32[]{:S(2)}, u32[]{:S(2)}) async-start(bf16[32,96,128]{2,1,0:T(8,128)(2,1)} %copy-done), calls=%async_computation.1 | async-start | bytes 1572864 | tf_op jit(solution)/shard_map/all_to_all | solution.py:619
  88.2 0.9 copy-start.1
  89.1 21.9 %all-to-all-start.2 = ((bf16[32,96,128]{2,1,0:T(8,128)(2,1)}), bf16[32,96,128]{2,1,0:T(8,128)(2,1)S(1)}, u32[]{:S(2)}, u32[]{:S(2)}) async-start(bf16[32,96,128]{2,1,0:T(8,128)(2,1)} %copy-done.1), calls=%async_computation.2 | async-start | bytes 1572864 | tf_op jit(solution)/shard_map/all_to_all | solution.py:619

commit v6 on v5

--- a/solution.py
+++ b/solution.py
@@ -318,7 +318,7 @@
     )(page_map, span_order, listed_count, listed_lanes)
 
 
-GROUPS = 4
+GROUPS = 2
 
 
 def blend_kernel(

time: 112 us -> 115 us (1.027)
  the two profiles are of different devices: /device:TPU:1 before, /device:TPU:193 now
where the time goes in v6:
time: 115 us; the launch traced here: 113 us
  Pallas kernels  53.3 us (46%)
  waiting for transfers between devices  36.7 us (32%)
  starting transfers between devices  20.3 us (18%)
  local copies, waits for them, and re-layouts  1.87 us (2%)
    all_to_all x3, waiting for transfers between devices, exchange(): return lax.all_to_all(blocks, 'shard', 0, 0)  36.7 us
    pallas_call x1, Pallas kernels, attend(): pl.pallas_call(attend_kernel, in_specs=[smem, smem, smem, vmem, vmem, vme...  33.4 us
    all_to_all x3, starting transfers between devices, exchange(): return lax.all_to_all(blocks, 'shard', 0, 0)  19.3 us
    pallas_call x1, Pallas kernels, plan(): pl.pallas_call(plan_kernel, in_specs=[smem, smem, smem, vmem], out_specs=...  8.61 us
    pallas_call x1, Pallas kernels, prepare(): pl.pallas_call(prepare_kernel, in_specs=[smem] * 5 + [vmem] + [anywhere]...  4.06 us
    pallas_call x1, Pallas kernels, blend(): pl.pallas_call(blend_kernel, in_specs=[smem, smem, smem, vmem, vmem], out...  3.77 us
    pallas_call x1, Pallas kernels, place_cache(): pl.pallas_call(place_cache_kernel, grid=(KV_HEADS,), in_specs=[pl.BlockSp...  2.62 us
  transfers between devices with their start and end apart: 4, of which 2 were waited for; matrix products, arithmetic and copies ran while one was open for 0% of the time, Pallas kernels for 39%

profile of v6, /device:TPU:193, one launch (start us, length us, event | category | flops | bytes accessed | tf_op | source)
XLA Modules:
  0.0 113.2 jit_solution(14411435873663515427)
XLA Ops:
  0.6 4.1 %prepare.1 = bf16[32,320,128]{2,1,0:T(8,128)(2,1)} custom-call(s32[1]{0:T(128)} %bitcast.me_ref, s32[352]{0:T(512)} %page_map.3, s32[8]{0:T(128)} %span_order.3, s32[1536]{0:T(1024)} %listed_index.1, f32[2,8,11]{2,1,0:T(8,128)} %bitcast.2, f32[1,128]{1,0:T(1,128)} %constant.8.clone.frequency, bf16[48,8192]{1,0:T(8,128)(2,1)} %queries_in.1, ...), custom_call_target="tpu_custom_call" | custom-call | flops 5000000000 | bytes 4300000 | tf_op jit(solution)/shard_map/prepare/pallas_call | solution.py:182
  4.7 0.0 copy-start.5
  4.7 0.0 copy-start.2
  4.7 0.0 copy-start.3
  4.7 0.0 copy-start.4
  4.8 7.9 %all-to-all-start = ((bf16[32,320,128]{2,1,0:T(8,128)(2,1)}), bf16[32,320,128]{2,1,0:T(8,128)(2,1)S(1)}, u32[]{:S(2)}, u32[]{:S(2)}) async-start(bf16[32,320,128]{2,1,0:T(8,128)(2,1)} %prepare.1), calls=%async_computation | async-start | bytes 5242880 | tf_op jit(solution)/shard_map/all_to_all | solution.py:619
  12.7 0.0 copy-done.5
  12.7 0.1 reshape.14
  12.8 0.0 copy-done.2
  12.8 0.1 fusion.listed_lanes
  12.8 0.0 copy-done.3
  12.8 0.0 copy-done.4
  12.8 8.6 %plan.1 = (s32[352]{0:T(512)S(1)}, s32[352]{0:T(512)S(1)}, s32[224]{0:T(256)S(1)}, s32[1]{0:T(128)}, s32[6,8,512]{2,1,0:T(8,128)S(1)}) custom-call(s32[352]{0:T(512)S(1)} %copy-done.3, s32[8]{0:T(128)S(1)} %copy-done.4, s32[32]{0:T(128)S(1)} %copy-done.2, s32[32,48]{1,0:T(8,128)S(1)} %fusion.listed_lanes), custom_call_target="tpu_custom_call" | custom-call | flops 8999999488 | bytes 3000000 | tf_op jit(solution)/shard_map/plan/pallas_call | solution.py:301
  21.4 25.1 %all-to-all-done.received = bf16[32,320,128]{2,1,0:T(8,128)(2,1)S(1)} async-done(((bf16[32,320,128]{2,1,0:T(8,128)(2,1)}), bf16[32,320,128]{2,1,0:T(8,128)(2,1)S(1)}, u32[]{:S(2)}, u32[]{:S(2)}) %all-to-all-start) | async-done | bytes 2621472 | tf_op jit(solution)/shard_map/all_to_all | solution.py:619
  46.6 3.8 %blend.1 = (bf16[45,128,128]{2,1,0:T(8,128)(2,1)}, bf16[32,96,128]{2,1,0:T(8,128)(2,1)S(1)}) custom-call(s32[1]{0:T(128)} %bitcast.me_ref, s32[352]{0:T(512)S(1)} %get-tuple-element.12.source, s32[352]{0:T(512)S(1)} %get-tuple-element.13.place, s32[32,48]{1,0:T(8,128)S(1)} %fusion.listed_lanes, bf16[32,320,128]{2,1,0:T(8,128)(2,1)S(1)} %all-to-all-done.received), custom_call_target="tpu_custom_call" | custom-call | flops 4000000000 | bytes 3000000 | tf_op jit(solution)/shard_map/blend/pallas_call | solution.py:397
  50.3 0.0 copy-start
  50.4 0.9 copy-done
  51.2 1.0 collective-permute-start
  52.2 3.7 %all-to-all-start.1 = ((bf16[32,96,128]{2,1,0:T(8,128)(2,1)}), bf16[32,96,128]{2,1,0:T(8,128)(2,1)S(1)}, u32[]{:S(2)}, u32[]{:S(2)}) async-start(bf16[32,96,128]{2,1,0:T(8,128)(2,1)} %copy-done), calls=%async_computation.1 | async-start | bytes 1572864 | tf_op jit(solution)/shard_map/all_to_all | solution.py:619
  55.9 0.0 collective-permute-done.other
  55.9 33.4 %attend.1 = bf16[32,96,128]{2,1,0:T(8,128)(2,1)S(1)} custom-call(s32[1]{0:T(128)} %bitcast.me_ref, s32[224]{0:T(256)S(1)} %get-tuple-element.17.tiles, s32[1]{0:T(128)} %get-tuple-element.18.block_count, s32[6,8,512]{2,1,0:T(8,128)S(1)} %get-tuple-element.19.positions, bf16[32,320,128]{2,1,0:T(8,128)(2,1)S(1)} %all-to-all-done.received, ...), custom_call_target="tpu_custom_call" | custom-call | flops 16000000000 | bytes 3000000 | tf_op jit(solution)/shard_map/attend/pallas_call | solution.py:548
  89.3 0.0 copy-start.1
  89.3 0.9 copy-done.1
  90.2 0.0 all-to-all-done.1.received
  90.2 7.7 %all-to-all-start.2 = ((bf16[32,96,128]{2,1,0:T(8,128)(2,1)}), bf16[32,96,128]{2,1,0:T(8,128)(2,1)S(1)}, u32[]{:S(2)}, u32[]{:S(2)}) async-start(bf16[32,96,128]{2,1,0:T(8,128)(2,1)} %copy-done.1), calls=%async_computation.2 | async-start | bytes 1572864 | tf_op jit(solution)/shard_map/all_to_all | solution.py:619
  97.9 2.6 %place_cache.1 = (bf16[11,16,1024]{2,1,0:T(8,128)(2,1)}, bf16[11,16,1024]{2,1,0:T(8,128)(2,1)}) custom-call(bf16[32,96,128]{2,1,0:T(8,128)(2,1)S(1)} %all-to-all-done.1.received), custom_call_target="tpu_custom_call" | custom-call | flops 2500000000 | bytes 3000000 | tf_op jit(solution)/shard_map/place_cache/pallas_call | solution.py:579
  100.5 11.6 %all-to-all-done.2.received = bf16[32,96,128]{2,1,0:T(8,128)(2,1)S(1)} async-done(((bf16[32,96,128]{2,1,0:T(8,128)(2,1)}), bf16[32,96,128]{2,1,0:T(8,128)(2,1)S(1)}, u32[]{:S(2)}, u32[]{:S(2)}) %all-to-all-start.2) | async-done | bytes 786464 | tf_op jit(solution)/shard_map/all_to_all | solution.py:619
  112.2 0.8 place_attended.1
Async XLA Ops:
  4.7 8.0 %copy-start.5 = (s32[1536]{0:T(1024)S(1)}, s32[1536]{0:T(1024)}, u32[]{:S(2)}) copy-start(s32[1536]{0:T(1024)} %listed_index.1) | copy-start | bytes 18436
  4.7 8.0 %copy-start.2 = (s32[32]{0:T(128)S(1)}, s32[32]{0:T(128)}, u32[]{:S(2)}) copy-start(s32[32]{0:T(128)} %listed_count.1) | copy-start | bytes 388
  4.7 8.1 %copy-start.3 = (s32[352]{0:T(512)S(1)}, s32[352]{0:T(512)}, u32[]{:S(2)}) copy-start(s32[352]{0:T(512)} %page_map.3) | copy-start | bytes 4228
  4.7 8.1 %copy-start.4 = (s32[8]{0:T(128)S(1)}, s32[8]{0:T(128)}, u32[]{:S(2)}) copy-start(s32[8]{0:T(128)} %span_order.3) | copy-start | bytes 100
  4.8 41.8 %all-to-all-start = ((bf16[32,320,128]{2,1,0:T(8,128)(2,1)}), bf16[32,320,128]{2,1,0:T(8,128)(2,1)S(1)}, u32[]{:S(2)}, u32[]{:S(2)}) async-start(bf16[32,320,128]{2,1,0:T(8,128)(2,1)} %prepare.1), calls=%async_computation | async-start | bytes 5242880 | tf_op jit(solution)/shard_map/all_to_all | solution.py:619
  50.3 0.9 copy-start
  51.2 4.7 %collective-permute-start = (bf16[45,128,128]{2,1,0:T(8,128)(2,1)}, bf16[45,128,128]{2,1,0:T(8,128)(2,1)}, u32[]{:S(2)}, u32[]{:S(2)}) collective-permute-start(bf16[45,128,128]{2,1,0:T(8,128)(2,1)} %get-tuple-element.20.mine), channel_id=1, source_target_pairs={{0,1},{1,0},{2,3},{3,2},{4,5},{5,4},{6,7},{7,6},{8,9},{9,8},{10,11... | collective-permute-start | bytes 4423688 | tf_op jit(solution)/shard_map/ppermute | solution.py:662
  52.2 38.0 %all-to-all-start.1 = ((bf16[32,96,128]{2,1,0:T(8,128)(2,1)}), bf16[32,96,128]{2,1,0:T(8,128)(2,1)S(1)}, u32[]{:S(2)}, u32[]{:S(2)}) async-start(bf16[32,96,128]{2,1,0:T(8,128)(2,1)} %copy-done), calls=%async_computation.1 | async-start | bytes 1572864 | tf_op jit(solution)/shard_map/all_to_all | solution.py:619
  89.3 0.9 copy-start.1
  90.2 21.9 %all-to-all-start.2 = ((bf16[32,96,128]{2,1,0:T(8,128)(2,1)}), bf16[32,96,128]{2,1,0:T(8,128)(2,1)S(1)}, u32[]{:S(2)}, u32[]{:S(2)}) async-start(bf16[32,96,128]{2,1,0:T(8,128)(2,1)} %copy-done.1), calls=%async_computation.2 | async-start | bytes 1572864 | tf_op jit(solution)/shard_map/all_to_all | solution.py:619
